TPU v7x, 32 devices: a whole 2x2x4 slice. The times are simulated.
32 devices in a mesh: groups: 2 (over y), pool: 8 (over z, x), tp: 2 (over core).
Axes of the slice: x: 2, y: 2, z: 4, core: 2. Of those that a mesh axis runs over, the one named last changes fastest.
Arguments:
- prompt_hidden: bfloat16 [8192, 256], P('pool', 'groups'), parts along dimension 1, may hold values from -6 to 6
- kv_weight: bfloat16 [2, 8192, 512], P(None, 'pool', 'tp'), may hold values from -0.0625 to 0.0625
- cache_kv: bfloat16 [2, 4096, 16, 512], P(None, ('groups', 'pool'), None, 'tp'), parts along dimension 1, may hold values from -6 to 6
- block_table: int32 [64, 64], P(('groups', 'pool')), parts along dimension 0, may hold values from 0 to 255, as said below
- cache_len: int32 [64], P(('groups', 'pool')), parts along dimension 0, may hold values from 1 to 1024, as said below
- page_request: int32 [16], P('groups'), parts along dimension 0, may hold values from 0 to 31, as said below
- prompt_len: int32 [64], P(('groups', 'pool')), parts along dimension 0, may hold values from 0 to 32, as said below
- query: bfloat16 [64, 4, 4096], P(('groups', 'pool'), None, 'tp'), parts along dimension 0, may hold values from -64 to 64
- new_kv: bfloat16 [2, 64, 4, 512], P(None, ('groups', 'pool'), None, 'tp'), parts along dimension 1, may hold values from -6 to 6
Outputs:
- attended: bfloat16 [64, 4, 4096], P(('groups', 'pool'), None, 'tp'), parts along dimension 0
There are 2 independent parts, one for each index of `groups`. A program takes and returns all parts, laid end to end along the dimension named above; an argument that names none is the same for every part. Nothing has to cross between parts.
Inputs may be any that keep to these rules, and one draw needn't show every extreme that they name: `block_table`: row r holds 64 distinct pages of its owner's pool, local numbers; the rows of one owner together use each of its 256 pages once. `cache_len`: at least one request has the full 64 * 16 cached tokens. `page_request`: Non-decreasing; request 0 has exactly the first 2 pages, every other request at most one page, and request 32 - 1 has one. `prompt_len`: zero for requests without prompt pages; otherwise more than 16 times one less than their page count and at most 16 times it; request 0 has exactly 32.
All inputs are finite; a program needn't handle non-finite values.
Results may differ from a plain program's by a relative error of at most 0.0059.
Values may be sent and summed in bfloat16 or wider, within the bound.
No kernel may reach another device: no remote copies, remote signals or barrier semaphores. Data moves between devices by JAX's collectives and lax.ppermute only.
A program may use at most 64 MiB of HBM per device.

v0:
```python
import jax
import jax.numpy as jnp
from jax import lax
from jax.sharding import PartitionSpec as P

HEADS_Q = 32
HEADS_KV = 4
HEAD_DIM = 128


def on_device(
    prompt_hidden,
    kv_weight,
    cache_kv,
    block_table,
    cache_len,
    page_request,
    prompt_len,
    query,
    new_kv,
):
    kv_local = kv_weight.shape[2]
    groups = kv_local // HEAD_DIM
    per_group = HEADS_Q // HEADS_KV
    page_size = cache_kv.shape[2]
    page_total = page_request.shape[0]
    kv_slab = jnp.concatenate((kv_weight[0], kv_weight[1]), axis=1)
    contract_dims = (((0,), (0,)), ((), ()))
    partial_value = lax.dot_general(
        prompt_hidden, kv_slab, contract_dims, preferred_element_type=jnp.float32
    )
    prompt_rows = lax.psum(partial_value, "pool").astype(jnp.bfloat16)
    local_reqs = query.shape[0]
    num_steps = query.shape[1]
    request_ids = lax.axis_index("pool") * local_reqs + jnp.arange(local_reqs, dtype=jnp.int32)
    first_page = jnp.sum((page_request[None, :] < request_ids[:, None]).astype(jnp.int32), axis=1)
    window_pages = page_total // 4 + local_reqs - 1
    begin_page = jnp.clip(first_page[0], 0, page_total - window_pages)
    window_tokens = window_pages * page_size
    window_rows = lax.dynamic_slice_in_dim(prompt_rows, begin_page * page_size, window_tokens, 0)
    window_owner = jnp.repeat(
        lax.dynamic_slice_in_dim(page_request, begin_page, window_pages, 0), page_size
    )
    token_index = begin_page * page_size + jnp.arange(window_tokens, dtype=jnp.int32)
    prompt_keys = window_rows[:, :kv_local].reshape(window_tokens, groups, HEAD_DIM)
    prompt_values = window_rows[:, kv_local:].reshape(window_tokens, groups, HEAD_DIM)
    prompt_mask = (window_owner[None, :] == request_ids[:, None]) & (
        token_index[None, :] - page_size * first_page[:, None] < prompt_len[:, None]
    )
    old_kv = cache_kv[:, block_table]
    span = old_kv.shape[2] * page_size
    old_kv = old_kv.reshape(2, local_reqs, span, groups, HEAD_DIM)
    old_mask = jnp.arange(span)[None, :] < cache_len[:, None]
    fresh_kv = new_kv.reshape(2, local_reqs, num_steps, groups, HEAD_DIM)
    queries = query.reshape(local_reqs, num_steps, groups, per_group, HEAD_DIM)
    causal = jnp.arange(num_steps)[None, :] <= jnp.arange(num_steps)[:, None]
    score_old = jnp.einsum(
        "rsgqd,rtgd->rsgqt", queries, old_kv[0], preferred_element_type=jnp.float32
    )
    score_prompt = jnp.einsum(
        "rsgqd,tgd->rsgqt", queries, prompt_keys, preferred_element_type=jnp.float32
    )
    score_new = jnp.einsum(
        "rsgqd,rugd->rsgqu", queries, fresh_kv[0], preferred_element_type=jnp.float32
    )
    full_mask = jnp.concatenate(
        [
            jnp.broadcast_to(old_mask[:, None, :], (local_reqs, num_steps, span)),
            jnp.broadcast_to(prompt_mask[:, None, :], (local_reqs, num_steps, window_tokens)),
            jnp.broadcast_to(causal[None, :, :], (local_reqs, num_steps, num_steps)),
        ],
        axis=2,
    )[:, :, None, None, :]
    scores = jnp.concatenate([score_old, score_prompt, score_new], axis=-1) * HEAD_DIM ** (-0.5)
    scores = jnp.where(full_mask, scores, -jnp.inf)
    row_max = jnp.max(scores, axis=-1, keepdims=True)
    shifted = jnp.exp(scores - row_max)
    weights = (shifted / jnp.sum(shifted, axis=-1, keepdims=True)).astype(jnp.bfloat16)
    outputs = jnp.einsum(
        "rsgqt,rtgd->rsgqd", weights[..., :span], old_kv[1], preferred_element_type=jnp.float32
    )
    outputs = outputs + jnp.einsum(
        "rsgqt,tgd->rsgqd",
        weights[..., span : span + window_tokens],
        prompt_values,
        preferred_element_type=jnp.float32,
    )
    outputs = outputs + jnp.einsum(
        "rsgqu,rugd->rsgqd",
        weights[..., span + window_tokens :],
        fresh_kv[1],
        preferred_element_type=jnp.float32,
    )
    return outputs.reshape(local_reqs, num_steps, groups * per_group * HEAD_DIM).astype(
        jnp.bfloat16
    )


def solution(mesh):
    in_specs = (
        P("pool", "groups"),
        P(None, "pool", "tp"),
        P(None, ("groups", "pool"), None, "tp"),
        P(("groups", "pool"), None),
        P(("groups", "pool")),
        P("groups"),
        P(("groups", "pool")),
        P(("groups", "pool"), None, "tp"),
        P(None, ("groups", "pool"), None, "tp"),
    )
    out_specs = P(("groups", "pool"), None, "tp")
    return jax.shard_map(
        on_device, mesh=mesh, in_specs=in_specs, out_specs=out_specs, check_vma=False
    )
```

profile of v0, /device:TPU:0, one launch (start us, length us, event | category | flops | bytes accessed | tf_op | source)
XLA Modules:
  0.0 70.0 jit_solution(12213779020985777881)
XLA Ops:
  0.0 0.0 copy-start
  0.0 0.7 %compare_select_fusion = s32[4,64]{1,0:T(4,128)S(1)} fusion(s32[4,64]{1,0:T(4,128)} %param.12), kind=kLoop, calls=%fused_computation.42 | loop fusion | flops 768 | bytes 2048 | tf_op jit(solution)/shard_map/select_n | solution.py:50
  0.7 0.1 reshape.137
  0.8 4.9 %gather_fusion = bf16[256,2,16,256]{3,2,1,0:T(8,128)(2,1)} fusion(bf16[2,256,16,256]{3,2,1,0:T(8,128)(2,1)} %param.11, s32[1024]{0:T(1024)S(1)} %pad_clamp_fusion), kind=kCustom, calls=%fused_computation | custom fusion | bytes 8389632 | tf_op jit(solution)/shard_map/gather | solution.py:50
  5.8 2.6 %copy.82 = bf16[4,64,2,16,256]{4,3,1,0,2:T(8,128)(2,1)S(1)} copy(bf16[4,64,2,16,256]{4,3,2,1,0:T(8,128)(2,1)} %bitcast.65) | data formatting | bytes 8388608 | tf_op jit(solution)/shard_map/gather | solution.py:50
  8.4 2.4 %fusion.43 = (bf16[1,4,64,16,256]{4,3,2,1,0:T(8,128)(2,1)}, bf16[1,4,64,16,256]{4,3,2,1,0:T(8,128)(2,1)}) fusion(bf16[2,4,64,16,256]{4,3,2,1,0:T(8,128)(2,1)S(1)} %bitcast.66), kind=kLoop, calls=%fused_computation.54 | loop fusion | bytes 8388608 | tf_op jit(solution)/shard_map/slice | solution.py:80
  10.8 0.0 copy-start.3
  10.8 2.6 %squeeze.20 = bf16[4,1024,2,128]{3,2,1,0:T(2,128)(2,1)S(1)} reshape(bf16[1,4,64,16,256]{4,3,2,1,0:T(8,128)(2,1)} %get-tuple-element.6) | data formatting | bytes 4194304 | tf_op jit(solution)/shard_map/squeeze | solution.py:58
  13.4 0.0 copy-done.3
  13.4 0.8 %fusion.7 = f32[4,4,2,8,1024]{4,3,1,2,0:T(8,128)S(1)} fusion(bf16[4,1024,2,128,1]{3,2,1,0,4:T(2,128)(2,1)S(1)} %bitcast.67, bf16[4,4,2,8,128]{4,3,2,1,0:T(8,128)(2,1)S(1)} %reshape.132), kind=kOutput, calls=%fused_computation.9 | convolution fusion | flops 67108864 | bytes 3211264 | tf_op jit(solution)/shard_map/rsgqd,rtgd->rsgqt/dot_general | solution.py:57
  14.2 0.0 copy-start.7
  14.2 1.3 %slice_bitcast_fusion.1 = (bf16[1024,256]{1,0:T(8,128)(2,1)S(1)}, bf16[1024,256]{1,0:T(8,128)(2,1)S(1)}) fusion(bf16[2,1024,256]{2,1,0:T(8,128)(2,1)} %param.10), kind=kLoop, calls=%fused_computation.30 | loop fusion | bytes 2097152 | tf_op jit(solution)/shard_map/squeeze | solution.py:27
  15.5 0.0 copy-start.4
  15.5 0.0 copy-done
  15.5 0.5 convolution_bitcast_fusion
  16.0 0.0 copy-start.5
  16.0 0.0 copy-start.6
  16.0 41.9 %all-reduce.1 = bf16[128,512]{0,1:T(8,128)(2,1)S(1)} all-reduce(f32[128,512]{0,1:T(8,128)S(1)} %convolution_bitcast_fusion), channel_id=1, replica_groups=mesh['groups'=2,'pool'=8,'tp'=2] {'pool'}, use_global_device_ids=true, to_apply=%region_1.0 | all-reduce | flops 65536 | bytes 393216 | tf_op jit(solution)/shard_map/psum | solution.py:32
  57.9 0.0 copy-done.7
  57.9 0.2 convert_reduce_fusion
  58.2 0.1 dynamic-slice_convert_fusion
  58.3 0.6 fusion.44
  58.9 0.2 convolution_bitcast_fusion.2
  59.1 0.0 copy-done.4
  59.1 0.1 convolution_bitcast_fusion.4
  59.2 0.3 concatenate.11
  59.5 0.0 copy-done.5
  59.5 0.1 iota_compare_fusion
  59.7 0.1 dynamic_slice.6
  59.7 0.1 broadcast_in_dim.20
  59.8 0.1 eq.19
  59.9 0.0 copy-done.6
  59.9 0.1 fusion.39
  60.0 0.7 %concatenate.9 = pred[4,4,1108]{2,1,0:T(4,128)(4,1)} concatenate(pred[4,4,1024]{2,1,0:T(4,128)(4,1)S(1)} %broadcast_in_dim.19, pred[4,4,80]{2,1,0:T(4,128)(4,1)S(1)} %broadcast_in_dim.21, pred[4,4,4]{2,1,0:T(4,128)(4,1)S(1)} %broadcast_in_dim.22), dimensions={2} | concatenate | bytes 35456 | tf_op jit(solution)/shard_map/concatenate | solution.py:66
  60.7 0.0 copy-start.2
  60.7 0.0 copy-start.1
  60.7 4.0 %fusion.45 = (f32[4,4,2,8]{3,1,2,0:T(4,128)S(1)}, f32[4,4,2,8,1108]{4,3,1,2,0:T(8,128)S(1)}) fusion(f32[4,4,2,8,1108]{4,3,1,2,0:T(8,128)S(1)} %concatenate.11, pred[4,4,1108]{2,1,0:T(4,128)(4,1)} %concatenate.9), kind=kOutput, calls=%fused_computation.56 | output fusion | flops 1135699 | bytes 2287936 | tf_op jit(solution)/shard_map/sub | solution.py:77
  64.7 0.1 divide_convert_fusion
  64.9 0.2 convolution_bitcast_fusion.3
  65.1 0.0 copy-done.2
  65.1 0.2 convolution_bitcast_fusion.1
  65.3 0.0 copy-done.1
  65.3 2.1 %squeeze.19 = bf16[4,1024,2,128]{3,2,1,0:T(2,128)(2,1)} reshape(bf16[1,4,64,16,256]{4,3,2,1,0:T(8,128)(2,1)S(1)} %copy-done.1) | data formatting | bytes 4194304 | tf_op jit(solution)/shard_map/squeeze | solution.py:80
  67.4 2.0 %fusion.19 = bf16[4,4,2,8,128]{4,3,1,2,0:T(8,128)(2,1)S(1)} fusion(f32[4,4,2,8,128]{4,3,1,2,0:T(8,128)S(1)} %convolution_bitcast_fusion.3, f32[4,4,2,8,128]{4,3,1,2,0:T(8,128)S(1)} %convolution_bitcast_fusion.1, bf16[4,1024,2,128,1]{3,2,1,0,4:T(2,128)(2,1)} %bitcast.68, bf16[4,4,2,8,1108]{4,3,1,2,0:T(8,128)(2,1)S(1)} %divide_convert_fusion), kind=kOutput, calls=%fused_computation.20 | convolution fusion | flops 67207168 | bytes 2949120 | tf_op jit(solution)/shard_map/rsgqt,rtgd->rsgqd/dot_general | solution.py:79
  69.4 0.6 convert_element_type.19
  (10 shorter events, 0.1 us)
Async XLA Ops:
  0.0 15.5 %copy-start = (bf16[1024,128]{1,0:T(8,128)(2,1)S(1)}, bf16[1024,128]{1,0:T(8,128)(2,1)}, u32[]{:S(2)}) copy-start(bf16[1024,128]{1,0:T(8,128)(2,1)} %param.9) | copy-start | bytes 786436
  10.8 2.6 %copy-start.3 = (bf16[4,4,2048]{2,1,0:T(4,128)(2,1)S(1)}, bf16[4,4,2048]{2,1,0:T(4,128)(2,1)}, u32[]{:S(2)}) copy-start(bf16[4,4,2048]{2,1,0:T(4,128)(2,1)} %param.16) | copy-start | bytes 196612
  14.2 43.7 %copy-start.7 = (s32[8]{0:T(128)S(1)}, s32[8]{0:T(128)}, u32[]{:S(2)}) copy-start(s32[8]{0:T(128)} %param.14) | copy-start | bytes 100
  15.5 43.6 %copy-start.4 = (bf16[2,4,4,256]{3,2,1,0:T(4,128)(2,1)S(1)}, bf16[2,4,4,256]{3,2,1,0:T(4,128)(2,1)}, u32[]{:S(2)}) copy-start(bf16[2,4,4,256]{3,2,1,0:T(4,128)(2,1)} %param.17) | copy-start | bytes 49156
  16.0 43.5 %copy-start.5 = (s32[4]{0:T(128)S(1)}, s32[4]{0:T(128)}, u32[]{:S(2)}) copy-start(s32[4]{0:T(128)} %param.13) | copy-start | bytes 52
  16.0 43.9 %copy-start.6 = (s32[4]{0:T(128)S(1)}, s32[4]{0:T(128)}, u32[]{:S(2)}) copy-start(s32[4]{0:T(128)} %param.15) | copy-start | bytes 52
  60.7 4.4 %copy-start.2 = (bf16[80,256]{0,1:T(8,128)(2,1)S(1)}, bf16[80,256]{0,1:T(8,128)(2,1)}, u32[]{:S(2)}) copy-start(bf16[80,256]{0,1:T(8,128)(2,1)} %get-tuple-element.9) | copy-start | bytes 122884
  60.7 4.6 %copy-start.1 = (bf16[1,4,64,16,256]{4,3,2,1,0:T(8,128)(2,1)S(1)}, bf16[1,4,64,16,256]{4,3,2,1,0:T(8,128)(2,1)}, u32[]{:S(2)}) copy-start(bf16[1,4,64,16,256]{4,3,2,1,0:T(8,128)(2,1)} %get-tuple-element.5) | copy-start | bytes 6291460
where the time goes:
time: 70.4 us; the launch traced here: 70 us
  blocking collectives  41.9 us (60%)
  local copies, waits for them, and re-layouts  18.7 us (27%)
  other arithmetic  5.24 us (7%)
  matrix products  3.94 us (6%)
    psum x1, blocking collectives, on_device(): prompt_rows = lax.psum(partial_value, 'pool').astype(jnp.bfloat16)  41.9 us
    gather x2, local copies, waits for them, and re-layouts, on_device(): old_kv = cache_kv[:, block_table]  7.53 us
    sub x1, other arithmetic, on_device(): shifted = jnp.exp(scores - row_max)  4.01 us
    squeeze x1, local copies, waits for them, and re-layouts, on_device(): old_kv[0]  2.58 us
    slice x1, local copies, waits for them, and re-layouts, on_device(): old_kv[1]  2.41 us
    squeeze x1, local copies, waits for them, and re-layouts, on_device(): old_kv[1]  2.08 us
    dot_general x1, matrix products, on_device(): jnp.einsum('rsgqt,rtgd->rsgqd', weights[..., :span], old_kv[1], preferred...  2 us

commit v1 on v0

v1 whole, which is shorter than its diff:
```python
import functools
import math

import jax
import jax.numpy as jnp
from jax import lax
from jax.experimental import pallas as pl
from jax.experimental.pallas import tpu as pltpu
from jax.sharding import PartitionSpec as P

HEAD_DIM = 128
PER_GROUP = 8
SCALE = HEAD_DIM**-0.5 * math.log2(math.e)
LOW = -1e30

VMEM = pl.BlockSpec(memory_space=pltpu.VMEM)
SMEM = pl.BlockSpec(memory_space=pltpu.SMEM)
HBM = pl.BlockSpec(memory_space=pltpu.HBM)


def in_hbm(*arrays):
    return [pltpu.with_memory_space_constraint(x, pltpu.HBM) for x in arrays]


def dot_nt(a, b):
    return lax.dot_general(a, b, (((1,), (1,)), ((), ())), preferred_element_type=jnp.float32)


def pages_before(owner_ref, request):
    count = jnp.int32(0)
    for p in range(owner_ref.shape[0]):
        count = count + jnp.where(owner_ref[p] < request, 1, 0)
    return count


def window_sizes(page_total, reqs):
    least = page_total // 4
    return list(range(least, min(page_total, least + reqs - 1) + 1))


def project_kernel(
    pieces, reqs, page, partners, hidden_ref, weight_ref, owner_hbm, own_ref, *rest
):
    if partners:
        send_ref, plan_ref, hidden_buf, weight_buf, owner_ref, sems, owner_sem = rest
    else:
        hidden_buf, weight_buf, owner_ref, sems, owner_sem = rest
    cols = weight_ref.shape[2]
    size = hidden_ref.shape[0] // pieces
    copies = []
    for i in range(pieces):
        at = pl.ds(i * size, size)
        copies.append(
            (
                pltpu.make_async_copy(hidden_ref.at[at], hidden_buf.at[at], sems.at[0, i]),
                pltpu.make_async_copy(weight_ref.at[0, at], weight_buf.at[0, at], sems.at[1, i]),
                pltpu.make_async_copy(weight_ref.at[1, at], weight_buf.at[1, at], sems.at[2, i]),
            )
        )
    owner_copy = pltpu.make_async_copy(owner_hbm, owner_ref, owner_sem)
    owner_copy.start()
    for group in copies:
        for copy in group:
            copy.start()
    owner_copy.wait()
    me = lax.axis_index("pool")
    for i, partner in enumerate(partners):
        first = pages_before(owner_ref, (me ^ partner) * reqs)
        plan_ref[i] = jnp.full(plan_ref.shape[1:], first, jnp.int32)
    totals = [0.0, 0.0]
    for i in range(pieces):
        for copy in copies[i]:
            copy.wait()
        at = slice(i * size, (i + 1) * size)
        for kind in range(2):
            totals[kind] = totals[kind] + lax.dot_general(
                hidden_buf[at],
                weight_buf[kind, at],
                (((0,), (0,)), ((), ())),
                preferred_element_type=jnp.float32,
            )
    for kind in range(2):
        own_ref[:, kind * cols : (kind + 1) * cols] = totals[kind].astype(jnp.bfloat16)
    if partners:
        begin = pl.multiple_of((1 - (me & 1)) * page, page)
        send_ref[...] = own_ref[pl.ds(begin, send_ref.shape[0]), :]


def project(hidden, weight, owner, reqs, page, partners):
    tokens, cols = hidden.shape[1], weight.shape[2]
    pieces = max(1, hidden.shape[0] // 256)
    out_shape = [jax.ShapeDtypeStruct((tokens, 2 * cols), jnp.bfloat16)]
    if partners:
        out_shape += [
            jax.ShapeDtypeStruct((tokens - page, 2 * cols), jnp.bfloat16),
            jax.ShapeDtypeStruct((len(partners), 8, HEAD_DIM), jnp.int32),
        ]
    return pl.pallas_call(
        functools.partial(project_kernel, pieces, reqs, page, partners),
        out_shape=out_shape,
        in_specs=[HBM] * 3,
        out_specs=[VMEM] * len(out_shape),
        scratch_shapes=[
            pltpu.VMEM(hidden.shape, jnp.bfloat16),
            pltpu.VMEM(weight.shape, jnp.bfloat16),
            pltpu.SMEM(owner.shape, jnp.int32),
            pltpu.SemaphoreType.DMA((3, pieces)),
            pltpu.SemaphoreType.DMA,
        ],
        compiler_params=pltpu.CompilerParams(vmem_limit_bytes=24 * 2**20),
        cost_estimate=pl.CostEstimate(
            flops=4 * hidden.size * cols,
            bytes_accessed=2 * (hidden.size + weight.size + tokens * 2 * cols),
            transcendentals=0,
        ),
        name="project",
    )(*in_hbm(hidden, weight, owner))


def pick_kernel(page, own_ref, got_ref, plan_ref, *rest):
    outs, total_ref = rest[:-1], rest[-1]
    tokens = own_ref.shape[0]
    begin = pl.multiple_of((lax.axis_index("pool") & 1) * page, page)
    at = pl.ds(begin, got_ref.shape[0])
    total_ref[...] = own_ref[...]
    total_ref[at, :] = (own_ref[at, :].astype(jnp.float32) + got_ref[...].astype(jnp.float32)).astype(
        jnp.bfloat16
    )
    total = total_ref[...]
    for i, out in enumerate(outs):
        rows = out.shape[0]
        shape = (rows // 8, 8, tokens)
        row = lax.broadcasted_iota(jnp.int32, shape, 0) * 8 + lax.broadcasted_iota(jnp.int32, shape, 1)
        col = lax.broadcasted_iota(jnp.int32, shape, 2)
        begin = jnp.minimum(plan_ref[i], (tokens - rows) // page)[None, :, :1] * page
        take = jnp.where(col - row == begin, 1.0, 0.0).reshape(rows, tokens).astype(jnp.bfloat16)
        out[...] = jnp.dot(take, total, preferred_element_type=jnp.float32).astype(jnp.bfloat16)


def pick(own, got, plan, rows, page):
    shape = jax.ShapeDtypeStruct((rows, own.shape[1]), jnp.bfloat16)
    count = plan.shape[0]
    return pl.pallas_call(
        functools.partial(pick_kernel, page),
        out_shape=[shape] * count,
        in_specs=[VMEM] * 3,
        out_specs=[VMEM] * count,
        scratch_shapes=[pltpu.VMEM(own.shape, jnp.bfloat16)],
        compiler_params=pltpu.CompilerParams(vmem_limit_bytes=24 * 2**20),
        cost_estimate=pl.CostEstimate(
            flops=2 * count * rows * own.size, bytes_accessed=4 * own.size, transcendentals=0
        ),
        name="pick",
    )(own, got, plan)


def cached_kernel(
    reqs, steps, groups, pages, owners,
    table_hbm, len_hbm, owner_hbm, prompt_hbm, cache_ref, query_hbm, new_hbm,
    q_out, o_out, m_out, l_out, bias_out, size_out,
    table_ref, len_ref, owner_ref, prompt_ref, query_ref, new_ref, kbuf, vbuf, qf, newf, sems, small,
):
    page = kbuf.shape[1]
    span = pages * page
    rows = groups * steps * PER_GROUP
    pieces = sems.shape[1]
    size = kbuf.shape[0] // pieces
    first_loads = [
        pltpu.make_async_copy(src, dst, small.at[i])
        for i, (src, dst) in enumerate(
            (
                (query_hbm, query_ref),
                (new_hbm, new_ref),
                (table_hbm, table_ref),
                (len_hbm, len_ref),
                (owner_hbm, owner_ref),
                (prompt_hbm, prompt_ref),
            )
        )
    ]
    copies = [
        [
            pltpu.make_async_copy(
                cache_ref.at[kind, pl.ds(i * size, size)],
                buf.at[pl.ds(i * size, size)],
                sems.at[kind, i],
            )
            for i in range(pieces)
        ]
        for kind, buf in enumerate((kbuf, vbuf))
    ]
    for copy in first_loads + copies[0] + copies[1]:
        copy.start()
    for copy in first_loads:
        copy.wait()

    me = lax.axis_index("pool")
    page_total = owner_ref.shape[0]
    begin = jnp.int32(0)
    if owners:
        least = window_sizes(page_total, reqs)[0]
        edges = [pages_before(owner_ref, o * reqs) for o in range(owners)] + [jnp.int32(page_total)]
        most = jnp.int32(least)
        for low, high in zip(edges, edges[1:]):
            most = jnp.maximum(most, high - low)
        size_out[0] = most - least
        begin = jnp.minimum(pages_before(owner_ref, me * reqs), page_total - most) * page
    else:
        size_out[0] = jnp.int32(0)
    col = lax.broadcasted_iota(jnp.int32, bias_out.shape[1:], 1) + begin
    for r in range(reqs):
        first = pages_before(owner_ref, me * reqs + r)
        last = pages_before(owner_ref, me * reqs + r + 1)
        end = jnp.minimum(first * page + prompt_ref[r], last * page)
        bias_out[r] = jnp.where((col >= first * page) & (col < end), 0.0, LOW)

    for r in range(reqs):
        for g in range(groups):
            for h in range(PER_GROUP):
                at = (g * PER_GROUP + h) * HEAD_DIM
                qf[pl.ds(r * rows + g * steps * PER_GROUP + h, steps, stride=PER_GROUP), :] = query_ref[
                    r, :, at : at + HEAD_DIM
                ].astype(jnp.float32)
    q_all = qf[...]
    row = lax.broadcasted_iota(jnp.int32, q_all.shape, 0)
    row_group = (row // (steps * PER_GROUP)) % groups
    q_out[...] = jnp.concatenate(
        [jnp.where(row_group == g, q_all, 0.0).astype(jnp.bfloat16) for g in range(groups)], axis=1
    )

    slot = HEAD_DIM // reqs
    newf[...] = jnp.zeros_like(newf)
    for kind in range(2):
        for r in range(reqs):
            newf[kind, r * slot : r * slot + steps, :] = new_ref[kind, r].astype(jnp.float32)
    new_k = newf[0].astype(jnp.bfloat16)
    new_v = newf[1].astype(jnp.bfloat16)

    for copy in copies[0]:
        copy.wait()
    scores, news, maxes = [], [], []
    for r in range(reqs):
        q = q_out[r * rows : (r + 1) * rows, :]
        s_new = dot_nt(q, new_k) * SCALE
        row = lax.broadcasted_iota(jnp.int32, s_new.shape, 0)
        col = lax.broadcasted_iota(jnp.int32, s_new.shape, 1) - r * slot
        step = (row // PER_GROUP) % steps
        s_new = jnp.where((col >= 0) & (col <= step), s_new, LOW)
        news.append(s_new)
        k = jnp.concatenate([kbuf[table_ref[r, j]] for j in range(pages)], axis=0)
        s = dot_nt(q, k) * SCALE
        col = lax.broadcasted_iota(jnp.int32, s.shape, 1)
        s = jnp.where(col < len_ref[r], s, LOW)
        scores.append(s)
        top = s_new
        for c in range(span // HEAD_DIM):
            top = jnp.maximum(top, s[:, c * HEAD_DIM : (c + 1) * HEAD_DIM])
        m = jnp.max(top, axis=1, keepdims=True)
        maxes.append(m)
        m_out[r * rows : (r + 1) * rows, :] = jnp.broadcast_to(m, (rows, HEAD_DIM))
    for copy in copies[1]:
        copy.wait()
    for r in range(reqs):
        p = jnp.exp2(scores[r] - maxes[r])
        p_new = jnp.exp2(news[r] - maxes[r])
        total = p_new
        for c in range(span // HEAD_DIM):
            total = total + p[:, c * HEAD_DIM : (c + 1) * HEAD_DIM]
        l_out[r * rows : (r + 1) * rows, :] = jnp.broadcast_to(
            jnp.sum(total, axis=1, keepdims=True), (rows, HEAD_DIM)
        )
        v = jnp.concatenate([vbuf[table_ref[r, j]] for j in range(pages)], axis=0)
        o = jnp.dot(p.astype(jnp.bfloat16), v, preferred_element_type=jnp.float32)
        o = o + jnp.dot(p_new.astype(jnp.bfloat16), new_v, preferred_element_type=jnp.float32)
        part = rows // groups
        for g in range(groups):
            o_out[r * rows + g * part : r * rows + (g + 1) * part, :] = o[
                g * part : (g + 1) * part, g * HEAD_DIM : (g + 1) * HEAD_DIM
            ]


def cached(table, length, owner, prompt_len, cache, query, new, tokens, owners):
    reqs, steps = query.shape[:2]
    groups = cache.shape[3] // HEAD_DIM
    pages, page = table.shape[1], cache.shape[2]
    rows = reqs * groups * steps * PER_GROUP
    flat = jax.ShapeDtypeStruct((rows, HEAD_DIM), jnp.float32)
    return pl.pallas_call(
        functools.partial(cached_kernel, reqs, steps, groups, pages, owners),
        out_shape=[
            jax.ShapeDtypeStruct((rows, groups * HEAD_DIM), jnp.bfloat16),
            flat,
            flat,
            flat,
            jax.ShapeDtypeStruct((reqs, 8, tokens), jnp.float32),
            jax.ShapeDtypeStruct((1,), jnp.int32),
        ],
        in_specs=[HBM] * 7,
        out_specs=[VMEM] * 5 + [SMEM],
        scratch_shapes=[
            pltpu.SMEM(table.shape, jnp.int32),
            pltpu.SMEM(length.shape, jnp.int32),
            pltpu.SMEM(owner.shape, jnp.int32),
            pltpu.SMEM(prompt_len.shape, jnp.int32),
            pltpu.VMEM(query.shape, jnp.bfloat16),
            pltpu.VMEM(new.shape, jnp.bfloat16),
            pltpu.VMEM(cache.shape[1:], jnp.bfloat16),
            pltpu.VMEM(cache.shape[1:], jnp.bfloat16),
            pltpu.VMEM((rows, HEAD_DIM), jnp.float32),
            pltpu.VMEM((2, HEAD_DIM, groups * HEAD_DIM), jnp.float32),
            pltpu.SemaphoreType.DMA((2, 4)),
            pltpu.SemaphoreType.DMA((6,)),
        ],
        compiler_params=pltpu.CompilerParams(vmem_limit_bytes=32 * 2**20),
        cost_estimate=pl.CostEstimate(
            flops=8 * rows * pages * page * HEAD_DIM,
            bytes_accessed=2 * cache.size,
            transcendentals=rows * pages * page,
        ),
        name="cached",
    )(*in_hbm(table, length, owner, prompt_len, cache, query, new))


def prompt_kernel(reqs, steps, groups, count, *refs):
    parts = refs[:count]
    q_ref, o_ref, m_ref, l_ref, bias_ref, out_ref, of = refs[count:]
    width = groups * HEAD_DIM
    rows = groups * steps * PER_GROUP
    tokens = bias_ref.shape[2]
    rows_kv = parts[0][...]
    if count > 1:
        total = rows_kv.astype(jnp.float32)
        for part in parts[1:]:
            total = total + part[...].astype(jnp.float32)
        rows_kv = total.astype(jnp.bfloat16)
    if rows_kv.shape[0] < tokens:
        rows_kv = jnp.concatenate(
            [rows_kv, jnp.zeros((tokens - rows_kv.shape[0], 2 * width), jnp.bfloat16)], axis=0
        )
    k, v = rows_kv[:, :width], rows_kv[:, width:]
    s_all = dot_nt(q_ref[...], k) * SCALE
    for r in range(reqs):
        at = slice(r * rows, (r + 1) * rows)
        s = (s_all[at].reshape(rows // 8, 8, tokens) + bias_ref[r][None]).reshape(rows, tokens)
        m_old = m_ref[at]
        m = jnp.maximum(m_old, jnp.max(s, axis=1, keepdims=True))
        alpha = jnp.exp2(m_old - m)
        p_new = jnp.exp2(s - m[:, :1])
        l = l_ref[at] * alpha + jnp.sum(p_new, axis=1, keepdims=True)
        pv = jnp.dot(p_new.astype(jnp.bfloat16), v, preferred_element_type=jnp.float32)
        part = rows // groups
        pv = jnp.concatenate(
            [pv[g * part : (g + 1) * part, g * HEAD_DIM : (g + 1) * HEAD_DIM] for g in range(groups)],
            axis=0,
        )
        of[at] = (o_ref[at] * alpha + pv) / l
    for r in range(reqs):
        for g in range(groups):
            for h in range(PER_GROUP):
                at = (g * PER_GROUP + h) * HEAD_DIM
                out_ref[r, :, at : at + HEAD_DIM] = of[
                    pl.ds(r * rows + g * steps * PER_GROUP + h, steps, stride=PER_GROUP), :
                ].astype(jnp.bfloat16)


def prompt(state, parts, query):
    reqs, steps = query.shape[:2]
    groups = parts[0].shape[1] // (2 * HEAD_DIM)
    q, o, m, l, bias = state
    return pl.pallas_call(
        functools.partial(prompt_kernel, reqs, steps, groups, len(parts)),
        out_shape=jax.ShapeDtypeStruct(query.shape, jnp.bfloat16),
        in_specs=[VMEM] * (5 + len(parts)),
        out_specs=VMEM,
        scratch_shapes=[pltpu.VMEM(o.shape, jnp.float32)],
        compiler_params=pltpu.CompilerParams(vmem_limit_bytes=24 * 2**20),
        name="prompt",
    )(*parts, q, o, m, l, bias)


def add_kernel(parts_ref, out_ref):
    total = parts_ref[0].astype(jnp.float32)
    for k in range(1, parts_ref.shape[0]):
        total = total + parts_ref[k].astype(jnp.float32)
    out_ref[...] = total.astype(jnp.bfloat16)


def add(parts):
    return pl.pallas_call(
        add_kernel,
        out_shape=jax.ShapeDtypeStruct(parts.shape[1:], jnp.bfloat16),
        in_specs=[VMEM],
        out_specs=VMEM,
        compiler_params=pltpu.CompilerParams(vmem_limit_bytes=24 * 2**20),
        name="add",
    )(parts)


def on_device(
    pool, prompt_hidden, kv_weight, cache_kv, block_table, cache_len, page_request, prompt_len, query, new_kv
):
    reqs, page, pages = query.shape[0], cache_kv.shape[2], page_request.shape[0]
    tokens = pages * page
    inputs = (block_table, cache_len, page_request, prompt_len, cache_kv, query, new_kv)
    if pool in (4, 8):
        partners = [0] + [p for p in (4, 6, 2) if p < pool]
        sizes = window_sizes(pages, reqs)
        own, send, plan = project(prompt_hidden, kv_weight, page_request, reqs, page, partners)
        got = lax.ppermute(send, "pool", [(i, i ^ 1) for i in range(pool)])
        *state, size = cached(*inputs, -(-sizes[-1] * page // HEAD_DIM) * HEAD_DIM, pool)

        def share(window, own, got, plan, state):
            cuts = pick(own, got, plan, window * page, page)
            parts = [cuts[0]] + [
                lax.ppermute(cut, "pool", [(i, i ^ p) for i in range(pool)])
                for cut, p in zip(cuts[1:], partners[1:])
            ]
            return prompt(state, parts, query)

        branches = [functools.partial(share, window) for window in sizes]
        return lax.switch(size[0], branches, own, got, plan, state)
    [own] = project(prompt_hidden, kv_weight, page_request, reqs, page, [])
    got = lax.all_to_all(own.reshape(pool, tokens // pool, -1), "pool", 0, 0, tiled=True)
    mine = add(got)
    shared = lax.all_to_all(jnp.broadcast_to(mine, got.shape), "pool", 0, 0, tiled=True)
    *state, _ = cached(*inputs, tokens, 0)
    return prompt(state, [shared.reshape(tokens, -1)], query)


def solution(mesh):
    in_specs = (
        P("pool", "groups"),
        P(None, "pool", "tp"),
        P(None, ("groups", "pool"), None, "tp"),
        P(("groups", "pool"), None),
        P(("groups", "pool")),
        P("groups"),
        P(("groups", "pool")),
        P(("groups", "pool"), None, "tp"),
        P(None, ("groups", "pool"), None, "tp"),
    )
    out_specs = P(("groups", "pool"), None, "tp")
    return jax.shard_map(
        functools.partial(on_device, mesh.shape["pool"]),
        mesh=mesh,
        in_specs=in_specs,
        out_specs=out_specs,
        check_vma=False,
    )
```

time: 70.4 us -> 19.1 us (0.27)
  blocking collectives: 41.9 us -> 0 us
  local copies, waits for them, and re-layouts: 18.7 us -> 0.62 us
  starting transfers between devices: 0 us -> 7.22 us
  Pallas kernels: 0 us -> 6.09 us
  other arithmetic: 5.24 us -> 0 us
  waiting for transfers between devices: 0 us -> 4.14 us
  matrix products: 3.94 us -> 0 us
    psum x1 -> x0, blocking collectives: 41.9 us -> none  [on_device(): prompt_rows = lax.psum(partial_value, 'pool').astype(jnp.bfloat16)]
    gather x2 -> x0, local copies, waits for them, and re-layouts: 7.53 us -> none  [on_device(): old_kv = cache_kv[:, block_table]]
    ppermute x0 -> x4, starting transfers between devices: none -> 7.22 us  [the longest x3 4.23 us: share(): lax.ppermute(cut, 'pool', [(i, i ^ p) for i in range(pool)])]
    pallas_call x0 -> x4, Pallas kernels: none -> 6.09 us  [the longest x1 3.56 us: cached(): pl.pallas_call(functools.partial(cached_kernel, reqs, steps, groups, page...]
    squeeze x3 -> x0, local copies, waits for them, and re-layouts: 5.94 us -> none  [the longest x1 2.58 us: on_device(): old_kv[0]]
    ppermute x0 -> x4, waiting for transfers between devices: none -> 4.14 us  [the longest x3 4.13 us: share(): lax.ppermute(cut, 'pool', [(i, i ^ p) for i in range(pool)])]
    sub x1 -> x0, other arithmetic: 4.01 us -> none  [on_device(): shifted = jnp.exp(scores - row_max)]
    dot_general x7 -> x0, matrix products: 3.94 us -> none  [the longest x1 2 us: on_device(): jnp.einsum('rsgqt,rtgd->rsgqd', weights[..., :span], old_kv[1], preferred...]
  transfers between devices with their start and end apart: 0 -> 4, of which waited for: 0 -> 2; matrix products, arithmetic and copies ran while one was open for 0% -> 0% of each run, Pallas kernels for 0% -> 19%
where the time goes in v1:
time: 19.1 us; the launch traced here: 18.8 us
  starting transfers between devices  7.22 us (38%)
  Pallas kernels  6.09 us (32%)
  waiting for transfers between devices  4.14 us (22%)
  between operations  0.69 us (4%)
  local copies, waits for them, and re-layouts  0.62 us (3%)
    ppermute x3, starting transfers between devices, share(): lax.ppermute(cut, 'pool', [(i, i ^ p) for i in range(pool)])  4.23 us
    ppermute x3, waiting for transfers between devices, share(): lax.ppermute(cut, 'pool', [(i, i ^ p) for i in range(pool)])  4.13 us
    pallas_call x1, Pallas kernels, cached(): pl.pallas_call(functools.partial(cached_kernel, reqs, steps, groups, page...  3.56 us
    ppermute x1, starting transfers between devices, on_device(): got = lax.ppermute(send, 'pool', [(i, i ^ 1) for i in range(pool)])  2.99 us
    pallas_call x1, Pallas kernels, project(): pl.pallas_call(functools.partial(project_kernel, pieces, reqs, page, part...  1.76 us
    unnamed x2, local copies, waits for them, and re-layouts  0.62 us
    pallas_call x1, Pallas kernels, prompt(): pl.pallas_call(functools.partial(prompt_kernel, reqs, steps, groups, len(...  0.51 us
  transfers between devices with their start and end apart: 4, of which 2 were waited for; matrix products, arithmetic and copies ran while one was open for 0% of the time, Pallas kernels for 19%

profile of v1, /device:TPU:0, one launch (start us, length us, event | category | flops | bytes accessed | tf_op | source)
XLA Modules:
  0.0 18.8 jit_solution(16247227208598203022)
XLA Ops:
  0.0 1.8 %project.1 = (bf16[128,512]{1,0:T(8,128)(2,1)S(1)}, bf16[112,512]{1,0:T(8,128)(2,1)S(1)}, s32[4,8,128]{2,1,0:T(8,128)S(1)}) custom-call(bf16[1024,128]{1,0:T(8,128)(2,1)} %hidden_ref.1, bf16[2,1024,256]{2,1,0:T(8,128)(2,1)} %weight_ref.1, s32[8]{0:T(128)} %owner_hbm.3), custom_call_target="tpu_custom_call" | custom-call | flops 134217728 | bytes 1441792 | tf_op jit(solution)/shard_map/project/pallas_call | solution.py:98
  1.8 3.0 %collective-permute-start.12 = (bf16[112,512]{1,0:T(8,128)(2,1)S(1)}, bf16[112,512]{1,0:T(8,128)(2,1)S(1)}, u32[]{:S(2)}, u32[]{:S(2)}) collective-permute-start(bf16[112,512]{1,0:T(8,128)(2,1)S(1)} %get-tuple-element.133), channel_id=1, source_target_pairs={{0,2},{2,0},{4,6},{6,4},{8,10},{10,8},{12,14},{14,12},{1,3},{3,1},... | collective-permute-start | bytes 344072 | tf_op jit(solution)/shard_map/ppermute | solution.py:409
  4.8 3.6 %cached.1 = (bf16[256,256]{1,0:T(8,128)(2,1)S(1)}, f32[256,128]{1,0:T(8,128)S(1)}, f32[256,128]{1,0:T(8,128)S(1)}, f32[256,128]{1,0:T(8,128)S(1)}, f32[4,8,128]{2,1,0:T(8,128)S(1)}, /*index=5*/s32[1]{0:T(128)}) custom-call(s32[4,64]{1,0:T(4,128)} %table_hbm.1, s32[4]{0:T(128)} %len_hbm.1, s32[8]{0:T(128)} %owner_hbm.3, s32[4]{0:T(128)} %prompt_hbm.1, ...), custom_call_target="tpu_custom_call" | custom-call | flops 268435456 | bytes 4194304 | tf_op jit(solution)/shard_map/cached/pallas_call | solution.py:288
  9.0 0.0 collective-permute-done.12
  9.0 9.2 %conditional.1 = (bf16[4,4,2048]{2,1,0:T(4,128)(2,1)S(1)}) conditional(s32[]{:T(128)} %bitcast, (bf16[128,512]{1,0:T(8,128)(2,1)S(1)}, bf16[112,512]{1,0:T(8,128)(2,1)S(1)}, s32[4,8,128]{2,1,0:T(8,128)S(1)}, bf16[256,256]{1,0:T(8,128)(2,1)S(1)}, f32[256,128]{1,0:T(8,128)S(1)}, /*index=5*/f32[256,128]{1,0:T(8,128)S(1)}, ...), branch_computations={%region_0.0_spmd, %region_1.0_spmd, %region_2.0_spmd, %region_3.0_... | conditional | flops 41943040 | bytes 1245312 | solution.py:421
  9.0 0.3 %pick.4 = (bf16[32,512]{1,0:T(8,128)(2,1)S(1)}, bf16[32,512]{1,0:T(8,128)(2,1)S(1)}, bf16[32,512]{1,0:T(8,128)(2,1)S(1)}, bf16[32,512]{1,0:T(8,128)(2,1)S(1)}) custom-call(bf16[128,512]{1,0:T(8,128)(2,1)S(1)} %get-tuple-element.72.own_ref, bf16[112,512]{1,0:T(8,128)(2,1)S(1)} %get-tuple-element.74.got_ref, s32[4,8,128]{2,1,0:T(8,128)S(1)} %get-tuple-element.76.plan_ref), custom_call_target="tpu_custom_call" | custom-call | flops 16777216 | bytes 262144 | tf_op jit(solution)/shard_map/cond/branch_0_fun/pick/pallas_call | solution.py:143
  9.3 2.7 %collective-permute-start = (bf16[32,512]{1,0:T(8,128)(2,1)S(1)}, bf16[32,512]{1,0:T(8,128)(2,1)S(1)}, u32[]{:S(2)}, u32[]{:S(2)}) collective-permute-start(bf16[32,512]{1,0:T(8,128)(2,1)S(1)} %get-tuple-element.78), channel_id=1, source_target_pairs={{0,8},{2,10},{4,12},{6,14},{8,0},{10,2},{12,4},{14,6},{1,9},{3,11}... | collective-permute-start | bytes 98312 | tf_op jit(solution)/shard_map/cond/branch_0_fun/ppermute | solution.py:415
  11.9 1.3 %collective-permute-start.1 = (bf16[32,512]{1,0:T(8,128)(2,1)S(1)}, bf16[32,512]{1,0:T(8,128)(2,1)S(1)}, u32[]{:S(2)}, u32[]{:S(2)}) collective-permute-start(bf16[32,512]{1,0:T(8,128)(2,1)S(1)} %get-tuple-element.79), channel_id=1, source_target_pairs={{0,12},{2,14},{4,8},{6,10},{8,4},{10,6},{12,0},{14,2},{1,13},{3,15... | collective-permute-start | bytes 98312 | tf_op jit(solution)/shard_map/cond/branch_0_fun/ppermute | solution.py:415
  13.3 0.2 %collective-permute-start.2 = (bf16[32,512]{1,0:T(8,128)(2,1)S(1)}, bf16[32,512]{1,0:T(8,128)(2,1)S(1)}, u32[]{:S(2)}, u32[]{:S(2)}) collective-permute-start(bf16[32,512]{1,0:T(8,128)(2,1)S(1)} %get-tuple-element.80), channel_id=1, source_target_pairs={{0,4},{2,6},{4,0},{6,2},{8,12},{10,14},{12,8},{14,10},{1,5},{3,7},... | collective-permute-start | bytes 98312 | tf_op jit(solution)/shard_map/cond/branch_0_fun/ppermute | solution.py:415
  13.5 0.6 %collective-permute-done.refs_1_ = bf16[32,512]{1,0:T(8,128)(2,1)S(1)} collective-permute-done((bf16[32,512]{1,0:T(8,128)(2,1)S(1)}, bf16[32,512]{1,0:T(8,128)(2,1)S(1)}, u32[]{:S(2)}, u32[]{:S(2)}) %collective-permute-start) | collective-permute-done | bytes 32800 | tf_op jit(solution)/shard_map/cond/branch_0_fun/ppermute | solution.py:415
  14.1 3.5 %collective-permute-done.1.refs_2_ = bf16[32,512]{1,0:T(8,128)(2,1)S(1)} collective-permute-done((bf16[32,512]{1,0:T(8,128)(2,1)S(1)}, bf16[32,512]{1,0:T(8,128)(2,1)S(1)}, u32[]{:S(2)}, u32[]{:S(2)}) %collective-permute-start.1) | collective-permute-done | bytes 32800 | tf_op jit(solution)/shard_map/cond/branch_0_fun/ppermute | solution.py:415
  17.6 0.0 collective-permute-done.2.refs_3_
  17.6 0.5 %prompt.4 = bf16[4,4,2048]{2,1,0:T(4,128)(2,1)S(1)} custom-call(bf16[32,512]{1,0:T(8,128)(2,1)S(1)} %get-tuple-element.77.refs_0_, bf16[32,512]{1,0:T(8,128)(2,1)S(1)} %collective-permute-done.refs_1_, bf16[32,512]{1,0:T(8,128)(2,1)S(1)} %collective-permute-done.1.refs_2_, bf16[32,512]{1,0:T(8,128)(2,1)S(1)} %collective-permute-done.2.refs_3_, ...), custom_call_target="tpu_custom_call" | custom-call | tf_op jit(solution)/shard_map/cond/branch_0_fun/prompt/pallas_call | solution.py:370
  18.2 0.0 copy-start
  18.2 0.6 %copy-done = bf16[4,4,2048]{2,1,0:T(4,128)(2,1)} copy-done((bf16[4,4,2048]{2,1,0:T(4,128)(2,1)}, bf16[4,4,2048]{2,1,0:T(4,128)(2,1)S(1)}, u32[]{:S(2)}) %copy-start) | copy-done | bytes 65560
Async XLA Ops:
  1.8 7.2 %collective-permute-start.12 = (bf16[112,512]{1,0:T(8,128)(2,1)S(1)}, bf16[112,512]{1,0:T(8,128)(2,1)S(1)}, u32[]{:S(2)}, u32[]{:S(2)}) collective-permute-start(bf16[112,512]{1,0:T(8,128)(2,1)S(1)} %get-tuple-element.133), channel_id=1, source_target_pairs={{0,2},{2,0},{4,6},{6,4},{8,10},{10,8},{12,14},{14,12},{1,3},{3,1},... | collective-permute-start | bytes 344072 | tf_op jit(solution)/shard_map/ppermute | solution.py:409
  9.3 4.9 %collective-permute-start = (bf16[32,512]{1,0:T(8,128)(2,1)S(1)}, bf16[32,512]{1,0:T(8,128)(2,1)S(1)}, u32[]{:S(2)}, u32[]{:S(2)}) collective-permute-start(bf16[32,512]{1,0:T(8,128)(2,1)S(1)} %get-tuple-element.78), channel_id=1, source_target_pairs={{0,8},{2,10},{4,12},{6,14},{8,0},{10,2},{12,4},{14,6},{1,9},{3,11}... | collective-permute-start | bytes 98312 | tf_op jit(solution)/shard_map/cond/branch_0_fun/ppermute | solution.py:415
  11.9 5.7 %collective-permute-start.1 = (bf16[32,512]{1,0:T(8,128)(2,1)S(1)}, bf16[32,512]{1,0:T(8,128)(2,1)S(1)}, u32[]{:S(2)}, u32[]{:S(2)}) collective-permute-start(bf16[32,512]{1,0:T(8,128)(2,1)S(1)} %get-tuple-element.79), channel_id=1, source_target_pairs={{0,12},{2,14},{4,8},{6,10},{8,4},{10,6},{12,0},{14,2},{1,13},{3,15... | collective-permute-start | bytes 98312 | tf_op jit(solution)/shard_map/cond/branch_0_fun/ppermute | solution.py:415
  13.3 4.4 %collective-permute-start.2 = (bf16[32,512]{1,0:T(8,128)(2,1)S(1)}, bf16[32,512]{1,0:T(8,128)(2,1)S(1)}, u32[]{:S(2)}, u32[]{:S(2)}) collective-permute-start(bf16[32,512]{1,0:T(8,128)(2,1)S(1)} %get-tuple-element.80), channel_id=1, source_target_pairs={{0,4},{2,6},{4,0},{6,2},{8,12},{10,14},{12,8},{14,10},{1,5},{3,7},... | collective-permute-start | bytes 98312 | tf_op jit(solution)/shard_map/cond/branch_0_fun/ppermute | solution.py:415
  18.2 0.6 %copy-start = (bf16[4,4,2048]{2,1,0:T(4,128)(2,1)}, bf16[4,4,2048]{2,1,0:T(4,128)(2,1)S(1)}, u32[]{:S(2)}) copy-start(bf16[4,4,2048]{2,1,0:T(4,128)(2,1)S(1)} %get-tuple-element.171) | copy-start | bytes 196612

commit v2 on v1

v2 whole, which is shorter than its diff:
```python
import functools
import math

import jax
import jax.numpy as jnp
from jax import lax
from jax.experimental import pallas as pl
from jax.experimental.pallas import tpu as pltpu
from jax.sharding import PartitionSpec as P

HEAD_DIM = 128
PER_GROUP = 8
SCALE = HEAD_DIM**-0.5 * math.log2(math.e)
LOW = -1e30

VMEM = pl.BlockSpec(memory_space=pltpu.VMEM)
SMEM = pl.BlockSpec(memory_space=pltpu.SMEM)
HBM = pl.BlockSpec(memory_space=pltpu.HBM)
ANY = pl.BlockSpec(memory_space=pl.ANY)


def in_hbm(*arrays):
    return [pltpu.with_memory_space_constraint(x, pltpu.HBM) for x in arrays]


def dot_nt(a, b):
    return lax.dot_general(a, b, (((1,), (1,)), ((), ())), preferred_element_type=jnp.float32)


def pages_before(owner_ref, request):
    count = jnp.int32(0)
    for p in range(owner_ref.shape[0]):
        count = count + jnp.where(owner_ref[p] < request, 1, 0)
    return count


def step_sizes(page_total, reqs):
    most = (page_total - 1, min(page_total, page_total // 4 + reqs - 1))
    usual = [(3, 2), (3, 3), (4, 3), (4, 4)]
    return [u for u in usual if u[0] < most[0] and u[1] <= most[1]] + [most]


def plan_steps(owner_ref, reqs, page, sizes, choice_ref, lists, plan_refs):
    me = lax.axis_index("pool")
    page_total = owner_ref.shape[0]
    for ref in lists:
        for p in range(page_total):
            ref[p] = jnp.int32(0)
    filled = [jnp.int32(0)] * 6
    counts = [jnp.int32(0)] * 2
    for p in range(page_total):
        owner = lax.div(owner_ref[p], jnp.int32(reqs))
        counts[0] = counts[0] + lax.shift_left(jnp.int32(1), 4 * (owner & 3))
        counts[1] = counts[1] + lax.shift_left(jnp.int32(1), 4 * owner)
        away = owner ^ me
        place = filled[0]
        for i in range(6):
            if i < 4:
                here, value = (away & 3) == i, jnp.int32(p)
            else:
                here, value = away == 4 * (5 - i), place
            lists[i][jnp.where(here, filled[i], page_total)] = value
            filled[i] = filled[i] + jnp.where(here, 1, 0)
    most = []
    for count, classes in zip(counts, (4, 8)):
        top = jnp.int32(0)
        for c in range(classes):
            top = jnp.maximum(top, lax.shift_right_logical(count, jnp.int32(4 * c)) & 15)
        most.append(top)
    choice = jnp.int32(len(sizes) - 1)
    for i in reversed(range(len(sizes) - 1)):
        fits = (most[0] <= sizes[i][0]) & (most[1] <= sizes[i][1])
        choice = jnp.where(fits, i, choice)
    choice_ref[0] = choice
    row = lax.broadcasted_iota(jnp.int32, (page, HEAD_DIM), 0)
    for ref, plan in zip(lists[4:], plan_refs):
        for j in range(plan.shape[0] // page):
            plan[j * page : (j + 1) * page, :] = ref[j] * page + row


def project_kernel(pieces, reqs, page, sizes, hidden_ref, weight_ref, owner_hbm, *rest):
    if sizes:
        count = 3 * len({size[0] for size in sizes})
        sends, (keep_ref, *plan_refs, choice_ref) = rest[:count], rest[count : count + 4]
        own_ref, hidden_buf, turned_buf, weight_buf, owner_ref, sems, small, *lists = rest[count + 4 :]
    else:
        own_ref, hidden_buf, turned_buf, weight_buf, owner_ref, sems, small = rest
    cols = weight_ref.shape[2]
    size = hidden_ref.shape[0] // pieces
    hidden_copy = pltpu.make_async_copy(hidden_ref, hidden_buf, small.at[0])
    owner_copy = pltpu.make_async_copy(owner_hbm, owner_ref, small.at[1])
    copies = []
    for i in range(pieces):
        at = pl.ds(i * size, size)
        copies.append(
            pltpu.make_async_copy(weight_ref.at[:, at], weight_buf.at[:, at], sems.at[i])
        )
    for copy in [hidden_copy, owner_copy] + copies:
        copy.start()
    owner_copy.wait()
    if sizes:
        plan_steps(owner_ref, reqs, page, sizes, choice_ref, lists, plan_refs)
    hidden_copy.wait()
    turned_buf[...] = hidden_buf[...].T
    totals = [0.0, 0.0]
    for i in range(pieces):
        copies[i].wait()
        at = slice(i * size, (i + 1) * size)
        for kind in range(2):
            totals[kind] = totals[kind] + jnp.dot(
                turned_buf[:, at], weight_buf[kind, at], preferred_element_type=jnp.float32
            )
    for kind in range(2):
        own_ref[:, kind * cols : (kind + 1) * cols] = totals[kind].astype(jnp.bfloat16)
    if sizes:

        def pack(largest, chosen):
            for j in range(largest):
                at = slice(j * page, (j + 1) * page)
                cuts = [
                    own_ref[pl.ds(pl.multiple_of(lists[i][j] * page, page), page), :]
                    for i in range(4)
                ]
                keep_ref[at, :] = cuts[0]
                for i, send in chosen:
                    if send.shape[0] > j * page:
                        send[at, :] = cuts[1 + i % 3]

        last = len(sizes) - 1
        all_sends = list(enumerate(sends))
        if last:
            pl.when(choice_ref[0] < last)(lambda: pack(max(u[0] for u in sizes[:last]), all_sends[:-3]))
        pl.when(choice_ref[0] == last)(lambda: pack(sizes[last][0], all_sends[-3:]))


def project(hidden, weight, owner, reqs, page, sizes):
    tokens, cols = hidden.shape[1], weight.shape[2]
    pieces = max(1, hidden.shape[0] // 128)
    rows = lambda n: jax.ShapeDtypeStruct((n * page, 2 * cols), jnp.bfloat16)
    scratch = [
        pltpu.VMEM(hidden.shape, jnp.bfloat16),
        pltpu.VMEM(hidden.shape[::-1], jnp.bfloat16),
        pltpu.VMEM(weight.shape, jnp.bfloat16),
        pltpu.SMEM(owner.shape, jnp.int32),
        pltpu.SemaphoreType.DMA((pieces,)),
        pltpu.SemaphoreType.DMA((2,)),
    ]
    if sizes:
        first, second = sizes[-1]
        plan = jax.ShapeDtypeStruct((second * page, HEAD_DIM), jnp.int32)
        out_shape = [rows(n) for n in sorted({size[0] for size in sizes}) for _ in range(3)]
        out_shape += [rows(first), plan, plan]
        out_specs = [VMEM] * len(out_shape) + [SMEM]
        out_shape += [pltpu.SMEM((1,), jnp.int32)]
        scratch = [pltpu.VMEM((tokens, 2 * cols), jnp.bfloat16)] + scratch
        scratch += [pltpu.SMEM((owner.shape[0] + 1,), jnp.int32)] * 6
    else:
        out_shape, out_specs = [rows(tokens // page)], [VMEM]
    return pl.pallas_call(
        functools.partial(project_kernel, pieces, reqs, page, sizes),
        out_shape=out_shape,
        in_specs=[HBM] * 3,
        out_specs=out_specs,
        scratch_shapes=scratch,
        compiler_params=pltpu.CompilerParams(vmem_limit_bytes=24 * 2**20),
        cost_estimate=pl.CostEstimate(
            flops=4 * hidden.size * cols,
            bytes_accessed=2 * (hidden.size + weight.size + tokens * 2 * cols),
            transcendentals=0,
        ),
        name="project",
    )(*in_hbm(hidden, weight, owner))


def fold_kernel(keep_ref, *refs):
    got, (send_plan, keep_plan, _, send_out, keep_out) = refs[:-5], refs[-5:]
    rows = got[0].shape[0]
    total = keep_ref[:rows].astype(jnp.float32)
    for ref in got:
        total = total + ref[...].astype(jnp.float32)
    pad = jnp.zeros((HEAD_DIM - rows, total.shape[1]), jnp.bfloat16)
    total = jnp.concatenate([total.astype(jnp.bfloat16), pad], axis=0)
    for plan, out in ((send_plan, send_out), (keep_plan, keep_out)):
        at = plan[: out.shape[0]]
        col = lax.broadcasted_iota(jnp.int32, at.shape, 1)
        take = jnp.where(at == col, 1.0, 0.0).astype(jnp.bfloat16)
        out[...] = jnp.dot(take, total, preferred_element_type=jnp.float32).astype(jnp.bfloat16)


def fold(keep, got, plans, rows, after):
    out = jax.ShapeDtypeStruct((rows, keep.shape[1]), jnp.bfloat16)
    return pl.pallas_call(
        fold_kernel,
        out_shape=[out, out],
        in_specs=[VMEM] * (3 + len(got)) + [ANY],
        out_specs=[VMEM] * 2,
        compiler_params=pltpu.CompilerParams(vmem_limit_bytes=24 * 2**20),
        cost_estimate=pl.CostEstimate(
            flops=4 * rows * keep.size, bytes_accessed=8 * keep.size, transcendentals=0
        ),
        name="fold",
    )(keep, *got, *plans, after)


def cached_kernel(
    reqs, steps, groups, pages, packed,
    table_hbm, len_hbm, owner_hbm, prompt_hbm, cache_ref, query_hbm, new_hbm, after_ref,
    q_out, o_out, m_out, l_out, bias_out,
    table_ref, len_ref, owner_ref, prompt_ref, query_ref, new_ref, kbuf, vbuf, qf, newf, sems, small,
):
    page = kbuf.shape[1]
    span = pages * page
    rows = groups * steps * PER_GROUP
    pieces = sems.shape[1]
    size = kbuf.shape[0] // pieces
    first_loads = [
        pltpu.make_async_copy(src, dst, small.at[i])
        for i, (src, dst) in enumerate(
            (
                (query_hbm, query_ref),
                (new_hbm, new_ref),
                (table_hbm, table_ref),
                (len_hbm, len_ref),
                (owner_hbm, owner_ref),
                (prompt_hbm, prompt_ref),
            )
        )
    ]
    copies = [
        [
            pltpu.make_async_copy(
                cache_ref.at[kind, pl.ds(i * size, size)],
                buf.at[pl.ds(i * size, size)],
                sems.at[kind, i],
            )
            for i in range(pieces)
        ]
        for kind, buf in enumerate((kbuf, vbuf))
    ]
    for copy in first_loads + copies[0] + copies[1]:
        copy.start()
    for copy in first_loads:
        copy.wait()

    me = lax.axis_index("pool")
    firsts = [pages_before(owner_ref, me * reqs + r) for r in range(reqs + 1)]
    begin = firsts[0] * page if packed else 0
    col = lax.broadcasted_iota(jnp.int32, bias_out.shape[1:], 1) + begin
    for r, (first, last) in enumerate(zip(firsts, firsts[1:])):
        end = jnp.minimum(first * page + prompt_ref[r], last * page)
        bias_out[r] = jnp.where((col >= first * page) & (col < end), 0.0, LOW)

    for r in range(reqs):
        for g in range(groups):
            for h in range(PER_GROUP):
                at = (g * PER_GROUP + h) * HEAD_DIM
                qf[pl.ds(r * rows + g * steps * PER_GROUP + h, steps, stride=PER_GROUP), :] = query_ref[
                    r, :, at : at + HEAD_DIM
                ].astype(jnp.float32)
    q_all = qf[...]
    row = lax.broadcasted_iota(jnp.int32, q_all.shape, 0)
    row_group = (row // (steps * PER_GROUP)) % groups
    q_out[...] = jnp.concatenate(
        [jnp.where(row_group == g, q_all, 0.0).astype(jnp.bfloat16) for g in range(groups)], axis=1
    )

    slot = HEAD_DIM // reqs
    newf[...] = jnp.zeros_like(newf)
    for kind in range(2):
        for r in range(reqs):
            newf[kind, r * slot : r * slot + steps, :] = new_ref[kind, r].astype(jnp.float32)
    new_k = newf[0].astype(jnp.bfloat16)
    new_v = newf[1].astype(jnp.bfloat16)

    for copy in copies[0]:
        copy.wait()
    scores, news, maxes = [], [], []
    for r in range(reqs):
        q = q_out[r * rows : (r + 1) * rows, :]
        s_new = dot_nt(q, new_k) * SCALE
        row = lax.broadcasted_iota(jnp.int32, s_new.shape, 0)
        col = lax.broadcasted_iota(jnp.int32, s_new.shape, 1) - r * slot
        step = (row // PER_GROUP) % steps
        s_new = jnp.where((col >= 0) & (col <= step), s_new, LOW)
        news.append(s_new)
        k = jnp.concatenate([kbuf[table_ref[r, j]] for j in range(pages)], axis=0)
        s = dot_nt(q, k) * SCALE
        col = lax.broadcasted_iota(jnp.int32, s.shape, 1)
        s = jnp.where(col < len_ref[r], s, LOW)
        scores.append(s)
        top = s_new
        for c in range(span // HEAD_DIM):
            top = jnp.maximum(top, s[:, c * HEAD_DIM : (c + 1) * HEAD_DIM])
        m = jnp.max(top, axis=1, keepdims=True)
        maxes.append(m)
        m_out[r * rows : (r + 1) * rows, :] = jnp.broadcast_to(m, (rows, HEAD_DIM))
    for copy in copies[1]:
        copy.wait()
    for r in range(reqs):
        p = jnp.exp2(scores[r] - maxes[r])
        p_new = jnp.exp2(news[r] - maxes[r])
        total = p_new
        for c in range(span // HEAD_DIM):
            total = total + p[:, c * HEAD_DIM : (c + 1) * HEAD_DIM]
        l_out[r * rows : (r + 1) * rows, :] = jnp.broadcast_to(
            jnp.sum(total, axis=1, keepdims=True), (rows, HEAD_DIM)
        )
        v = jnp.concatenate([vbuf[table_ref[r, j]] for j in range(pages)], axis=0)
        o = jnp.dot(p.astype(jnp.bfloat16), v, preferred_element_type=jnp.float32)
        o = o + jnp.dot(p_new.astype(jnp.bfloat16), new_v, preferred_element_type=jnp.float32)
        part = rows // groups
        for g in range(groups):
            o_out[r * rows + g * part : r * rows + (g + 1) * part, :] = o[
                g * part : (g + 1) * part, g * HEAD_DIM : (g + 1) * HEAD_DIM
            ]


def cached(table, length, owner, prompt_len, cache, query, new, tokens, packed, after):
    reqs, steps = query.shape[:2]
    groups = cache.shape[3] // HEAD_DIM
    pages, page = table.shape[1], cache.shape[2]
    rows = reqs * groups * steps * PER_GROUP
    flat = jax.ShapeDtypeStruct((rows, HEAD_DIM), jnp.float32)
    return pl.pallas_call(
        functools.partial(cached_kernel, reqs, steps, groups, pages, packed),
        out_shape=[
            jax.ShapeDtypeStruct((rows, groups * HEAD_DIM), jnp.bfloat16),
            flat,
            flat,
            flat,
            jax.ShapeDtypeStruct((reqs, 8, tokens), jnp.float32),
        ],
        in_specs=[HBM] * 7 + [ANY],
        out_specs=[VMEM] * 5,
        scratch_shapes=[
            pltpu.SMEM(table.shape, jnp.int32),
            pltpu.SMEM(length.shape, jnp.int32),
            pltpu.SMEM(owner.shape, jnp.int32),
            pltpu.SMEM(prompt_len.shape, jnp.int32),
            pltpu.VMEM(query.shape, jnp.bfloat16),
            pltpu.VMEM(new.shape, jnp.bfloat16),
            pltpu.VMEM(cache.shape[1:], jnp.bfloat16),
            pltpu.VMEM(cache.shape[1:], jnp.bfloat16),
            pltpu.VMEM((rows, HEAD_DIM), jnp.float32),
            pltpu.VMEM((2, HEAD_DIM, groups * HEAD_DIM), jnp.float32),
            pltpu.SemaphoreType.DMA((2, 4)),
            pltpu.SemaphoreType.DMA((6,)),
        ],
        compiler_params=pltpu.CompilerParams(vmem_limit_bytes=32 * 2**20),
        cost_estimate=pl.CostEstimate(
            flops=8 * rows * pages * page * HEAD_DIM,
            bytes_accessed=2 * cache.size,
            transcendentals=rows * pages * page,
        ),
        name="cached",
    )(*in_hbm(table, length, owner, prompt_len, cache, query, new), after)


def prompt_kernel(reqs, steps, groups, count, *refs):
    parts = refs[:count]
    q_ref, o_ref, m_ref, l_ref, bias_ref, out_hbm, out_ref, of, sems = refs[count:]
    width = groups * HEAD_DIM
    rows = groups * steps * PER_GROUP
    tokens = bias_ref.shape[2]
    rows_kv = parts[0][...]
    if count > 1:
        total = rows_kv.astype(jnp.float32)
        for part in parts[1:]:
            total = total + part[...].astype(jnp.float32)
        rows_kv = total.astype(jnp.bfloat16)
    if rows_kv.shape[0] < tokens:
        rows_kv = jnp.concatenate(
            [rows_kv, jnp.zeros((tokens - rows_kv.shape[0], 2 * width), jnp.bfloat16)], axis=0
        )
    k, v = rows_kv[:, :width], rows_kv[:, width:]
    s = (dot_nt(q_ref[...], k) * SCALE).reshape(reqs, rows // 8, 8, tokens) + bias_ref[...][:, None]
    s = s.reshape(reqs * rows, tokens)
    m_old = m_ref[...]
    m = jnp.maximum(m_old, jnp.max(s, axis=1, keepdims=True))
    alpha = jnp.exp2(m_old - m)
    p_new = jnp.exp2(s - m[:, :1])
    l = l_ref[...] * alpha + jnp.sum(p_new, axis=1, keepdims=True)
    pv = jnp.dot(p_new.astype(jnp.bfloat16), v, preferred_element_type=jnp.float32)
    part = rows // groups
    pv = pv.reshape(reqs, groups, part, width)
    pv = jnp.stack([pv[:, g, :, g * HEAD_DIM : (g + 1) * HEAD_DIM] for g in range(groups)], axis=1)
    of[...] = (o_ref[...] * alpha + pv.reshape(reqs * rows, HEAD_DIM)) / l
    copies = []
    for r in range(reqs):
        for g in range(groups):
            for h in range(PER_GROUP):
                at = (g * PER_GROUP + h) * HEAD_DIM
                out_ref[r, :, at : at + HEAD_DIM] = of[
                    pl.ds(r * rows + g * steps * PER_GROUP + h, steps, stride=PER_GROUP), :
                ].astype(jnp.bfloat16)
        copies.append(pltpu.make_async_copy(out_ref.at[r], out_hbm.at[r], sems.at[r]))
        copies[r].start()
    for copy in copies:
        copy.wait()


def prompt(state, parts, query):
    reqs, steps = query.shape[:2]
    groups = parts[0].shape[1] // (2 * HEAD_DIM)
    q, o, m, l, bias = state
    return pl.pallas_call(
        functools.partial(prompt_kernel, reqs, steps, groups, len(parts)),
        out_shape=pltpu.HBM(query.shape, jnp.bfloat16),
        in_specs=[VMEM] * (5 + len(parts)),
        out_specs=HBM,
        scratch_shapes=[
            pltpu.VMEM(query.shape, jnp.bfloat16),
            pltpu.VMEM(o.shape, jnp.float32),
            pltpu.SemaphoreType.DMA((reqs,)),
        ],
        compiler_params=pltpu.CompilerParams(vmem_limit_bytes=24 * 2**20),
        name="prompt",
    )(*parts, q, o, m, l, bias)


def add_kernel(parts_ref, out_ref):
    total = parts_ref[0].astype(jnp.float32)
    for k in range(1, parts_ref.shape[0]):
        total = total + parts_ref[k].astype(jnp.float32)
    out_ref[...] = total.astype(jnp.bfloat16)


def add(parts):
    return pl.pallas_call(
        add_kernel,
        out_shape=jax.ShapeDtypeStruct(parts.shape[1:], jnp.bfloat16),
        in_specs=[VMEM],
        out_specs=VMEM,
        compiler_params=pltpu.CompilerParams(vmem_limit_bytes=24 * 2**20),
        name="add",
    )(parts)


def on_device(
    pool, prompt_hidden, kv_weight, cache_kv, block_table, cache_len, page_request, prompt_len, query, new_kv
):
    reqs, page, pages = query.shape[0], cache_kv.shape[2], page_request.shape[0]
    tokens = pages * page
    inputs = (block_table, cache_len, page_request, prompt_len, cache_kv, query, new_kv)
    if pool == 8 and pages <= 8:
        sizes = step_sizes(pages, reqs)
        firsts = sorted({size[0] for size in sizes})
        outs = project(prompt_hidden, kv_weight, page_request, reqs, page, sizes)
        sends, (keep, *plans, choice) = outs[: 3 * len(firsts)], outs[3 * len(firsts) :]

        def share(size, sends, keep, plans, inputs):
            def trade(x, bits):
                return lax.ppermute(x, "pool", [(i, i ^ bits) for i in range(pool)])

            at = 3 * firsts.index(size[0])
            got = [trade(sends[at + bits - 1], bits) for bits in (3, 1, 2)]
            state = cached(*inputs, HEAD_DIM, True, keep)
            send, mine = fold(keep, got, plans, size[1] * page, state[2])
            return prompt(state, [mine, trade(send, 4)], query)

        branches = [functools.partial(share, size) for size in sizes]
        choice = lax.optimization_barrier(choice.reshape(()))
        return lax.switch(choice, branches, sends, keep, plans, inputs)
    [own] = project(prompt_hidden, kv_weight, page_request, reqs, page, [])
    got = lax.all_to_all(own.reshape(pool, tokens // pool, -1), "pool", 0, 0, tiled=True)
    mine = add(got)
    shared = lax.all_to_all(jnp.broadcast_to(mine, got.shape), "pool", 0, 0, tiled=True)
    state = cached(*inputs, tokens, False, mine)
    return prompt(state, [shared.reshape(tokens, -1)], query)


def solution(mesh):
    in_specs = (
        P("pool", "groups"),
        P(None, "pool", "tp"),
        P(None, ("groups", "pool"), None, "tp"),
        P(("groups", "pool"), None),
        P(("groups", "pool")),
        P("groups"),
        P(("groups", "pool")),
        P(("groups", "pool"), None, "tp"),
        P(None, ("groups", "pool"), None, "tp"),
    )
    out_specs = P(("groups", "pool"), None, "tp")
    return jax.shard_map(
        functools.partial(on_device, mesh.shape["pool"]),
        mesh=mesh,
        in_specs=in_specs,
        out_specs=out_specs,
        check_vma=False,
    )
```

time: 19.1 us -> 17.6 us (0.921); the launches traced: 18.8 us -> 17.9 us
  between operations: 0.69 us -> 0.01 us
  local copies, waits for them, and re-layouts: 0.62 us -> 0 us
  Pallas kernels: 6.09 us -> 6.62 us
  waiting for transfers between devices: 4.14 us -> 3.89 us
    pallas_call x1, Pallas kernels: 0.51 us -> 1.17 us  [prompt(): pl.pallas_call(functools.partial(prompt_kernel, reqs, steps, groups, len(...]
    unnamed x2 -> x0, local copies, waits for them, and re-layouts: 0.62 us -> none
    pallas_call x1, Pallas kernels: 3.56 us -> 3.17 us  [cached(): pl.pallas_call(functools.partial(cached_kernel, reqs, steps, groups, page...]
    pallas_call x2, Pallas kernels: 2.02 us -> 2.28 us  [the longest x1 2.1 us: project(): pl.pallas_call(functools.partial(project_kernel, pieces, reqs, page, size...]
    ppermute x4, waiting for transfers between devices: 4.14 us -> 3.89 us  [trade(): return lax.ppermute(x, 'pool', [(i, i ^ bits) for i in range(pool)])]
  transfers between devices with their start and end apart: 4 -> 4, of which waited for: 2 -> 3; matrix products, arithmetic and copies ran while one was open for 0% -> 0% of each run, Pallas kernels for 19% -> 18%
where the time goes in v2:
time: 17.6 us; the launch traced here: 17.9 us
  starting transfers between devices  7.31 us (42%)
  Pallas kernels  6.62 us (38%)
  waiting for transfers between devices  3.89 us (22%)
    ppermute x4, starting transfers between devices, trade(): return lax.ppermute(x, 'pool', [(i, i ^ bits) for i in range(pool)])  7.31 us
    ppermute x4, waiting for transfers between devices, trade(): return lax.ppermute(x, 'pool', [(i, i ^ bits) for i in range(pool)])  3.89 us
    pallas_call x1, Pallas kernels, cached(): pl.pallas_call(functools.partial(cached_kernel, reqs, steps, groups, page...  3.17 us
    pallas_call x1, Pallas kernels, project(): pl.pallas_call(functools.partial(project_kernel, pieces, reqs, page, size...  2.1 us
    pallas_call x1, Pallas kernels, prompt(): pl.pallas_call(functools.partial(prompt_kernel, reqs, steps, groups, len(...  1.17 us
  transfers between devices with their start and end apart: 4, of which 3 were waited for; matrix products, arithmetic and copies ran while one was open for 0% of the time, Pallas kernels for 18%

profile of v2, /device:TPU:0, one launch (start us, length us, event | category | flops | bytes accessed | tf_op | source)
XLA Modules:
  0.0 17.9 jit_solution(15881322505361959718)
XLA Ops:
  0.0 2.1 %project.1 = (bf16[48,512]{1,0:T(8,128)(2,1)S(1)}, bf16[48,512]{1,0:T(8,128)(2,1)S(1)}, bf16[48,512]{1,0:T(8,128)(2,1)S(1)}, bf16[64,512]{1,0:T(8,128)(2,1)S(1)}...) custom-call(bf16[1024,128]{1,0:T(8,128)(2,1)} %hidden_ref.1, ...), custom_call_target="tpu_custom_call" | custom-call | flops 134217728 | bytes 1441792 | tf_op jit(solution)/shard_map/project/pallas_call | solution.py:159
  2.1 15.8 %conditional.1 = (bf16[4,4,2048]{2,1,0:T(4,128)(2,1)}) conditional(s32[]{:T(128)} %clamp.3, (bf16[48,512]{1,0:T(8,128)(2,1)S(1)}, bf16[48,512]{1,0:T(8,128)(2,1)S(1)}, bf16[48,512]{1,0:T(8,128)(2,1)S(1)}, s32[4,64]{1,0:T(4,128)}, s32[4]{0:T(128)}, /*index=5*/s32[8]{0:T(128)}, s32[4]{0:T(128)}, ...), branch_computations={%region_0.0_spmd, %region_1.0_spmd, %region_2.0_spmd, %region_3.0_... | conditional | flops 286785536 | bytes 6357160 | solution.py:463
  2.1 4.0 %collective-permute-start.8 = (bf16[64,512]{1,0:T(8,128)(2,1)S(1)}, bf16[64,512]{1,0:T(8,128)(2,1)S(1)}, u32[]{:S(2)}, u32[]{:S(2)}) collective-permute-start(bf16[64,512]{1,0:T(8,128)(2,1)S(1)} %get-tuple-element.182), channel_id=1, source_target_pairs={{0,6},{2,4},{4,2},{6,0},{8,14},{10,12},{12,10},{14,8},{1,7},{3,5},... | collective-permute-start | bytes 196616 | tf_op jit(solution)/shard_map/cond/branch_2_fun/ppermute | solution.py:453
  6.2 0.5 %collective-permute-start.9 = (bf16[64,512]{1,0:T(8,128)(2,1)S(1)}, bf16[64,512]{1,0:T(8,128)(2,1)S(1)}, u32[]{:S(2)}, u32[]{:S(2)}) collective-permute-start(bf16[64,512]{1,0:T(8,128)(2,1)S(1)} %get-tuple-element.183), channel_id=1, source_target_pairs={{0,2},{2,0},{4,6},{6,4},{8,10},{10,8},{12,14},{14,12},{1,3},{3,1},... | collective-permute-start | bytes 196616 | tf_op jit(solution)/shard_map/cond/branch_2_fun/ppermute | solution.py:453
  6.7 0.1 collective-permute-start.10
  6.8 3.2 %cached.7 = (bf16[256,256]{1,0:T(8,128)(2,1)S(1)}, f32[256,128]{1,0:T(8,128)S(1)}, f32[256,128]{1,0:T(8,128)S(1)}, f32[256,128]{1,0:T(8,128)S(1)}, f32[4,8,128]{2,1,0:T(8,128)S(1)}) custom-call(s32[4,64]{1,0:T(4,128)} %get-tuple-element.187.table_hbm, s32[4]{0:T(128)} %get-tuple-element.188.len_hbm, s32[8]{0:T(128)} %get-tuple-element.189.owner_hbm, ...), custom_call_target="tpu_custom_call" | custom-call | flops 268435456 | bytes 4194304 | tf_op jit(solution)/shard_map/cond/branch_2_fun/cached/pallas_call | solution.py:324
  10.0 0.0 collective-permute-done.8.refs_0_
  10.0 0.4 %collective-permute-done.9.refs_1_ = bf16[64,512]{1,0:T(8,128)(2,1)S(1)} collective-permute-done((bf16[64,512]{1,0:T(8,128)(2,1)S(1)}, bf16[64,512]{1,0:T(8,128)(2,1)S(1)}, u32[]{:S(2)}, u32[]{:S(2)}) %collective-permute-start.9) | collective-permute-done | bytes 65568 | tf_op jit(solution)/shard_map/cond/branch_2_fun/ppermute | solution.py:453
  10.4 0.5 %collective-permute-done.10.refs_2_ = bf16[64,512]{1,0:T(8,128)(2,1)S(1)} collective-permute-done((bf16[64,512]{1,0:T(8,128)(2,1)S(1)}, bf16[64,512]{1,0:T(8,128)(2,1)S(1)}, u32[]{:S(2)}, u32[]{:S(2)}) %collective-permute-start.10) | collective-permute-done | bytes 65568 | tf_op jit(solution)/shard_map/cond/branch_2_fun/ppermute | solution.py:453
  10.9 0.2 %fold.7 = (bf16[48,512]{1,0:T(8,128)(2,1)S(1)}, bf16[48,512]{1,0:T(8,128)(2,1)S(1)}) custom-call(bf16[112,512]{1,0:T(8,128)(2,1)S(1)} %get-tuple-element.181.after_ref.keep_ref, bf16[64,512]{1,0:T(8,128)(2,1)S(1)} %collective-permute-done.8.refs_0_, bf16[64,512]{1,0:T(8,128)(2,1)S(1)} %collective-permute-done.9.refs_1_, ...), custom_call_target="tpu_custom_call" | custom-call | flops 11010048 | bytes 458752 | tf_op jit(solution)/shard_map/cond/branch_2_fun/fold/pallas_call | solution.py:192
  11.1 2.7 %collective-permute-start.11 = (bf16[48,512]{1,0:T(8,128)(2,1)S(1)}, bf16[48,512]{1,0:T(8,128)(2,1)S(1)}, u32[]{:S(2)}, u32[]{:S(2)}) collective-permute-start(bf16[48,512]{1,0:T(8,128)(2,1)S(1)} %get-tuple-element.196), channel_id=1, source_target_pairs={{0,8},{2,10},{4,12},{6,14},{8,0},{10,2},{12,4},{14,6},{1,9},{3,11}... | collective-permute-start | bytes 147464 | tf_op jit(solution)/shard_map/cond/branch_2_fun/ppermute | solution.py:453
  13.8 2.9 %collective-permute-done.11.refs_1_ = bf16[48,512]{1,0:T(8,128)(2,1)S(1)} collective-permute-done((bf16[48,512]{1,0:T(8,128)(2,1)S(1)}, bf16[48,512]{1,0:T(8,128)(2,1)S(1)}, u32[]{:S(2)}, u32[]{:S(2)}) %collective-permute-start.11) | collective-permute-done | bytes 49184 | tf_op jit(solution)/shard_map/cond/branch_2_fun/ppermute | solution.py:453
  16.7 1.2 %prompt.7 = bf16[4,4,2048]{2,1,0:T(4,128)(2,1)} custom-call(bf16[48,512]{1,0:T(8,128)(2,1)S(1)} %get-tuple-element.195.refs_0_, bf16[48,512]{1,0:T(8,128)(2,1)S(1)} %collective-permute-done.11.refs_1_, bf16[256,256]{1,0:T(8,128)(2,1)S(1)} %get-tuple-element.197.refs_2_, f32[256,128]{1,0:T(8,128)S(1)} %get-tuple-element.198.refs_3_, ...), custom_call_target="tpu_custom_call" | custom-call | tf_op jit(solution)/shard_map/cond/branch_2_fun/prompt/pallas_call | solution.py:406
Async XLA Ops:
  2.1 7.8 %collective-permute-start.8 = (bf16[64,512]{1,0:T(8,128)(2,1)S(1)}, bf16[64,512]{1,0:T(8,128)(2,1)S(1)}, u32[]{:S(2)}, u32[]{:S(2)}) collective-permute-start(bf16[64,512]{1,0:T(8,128)(2,1)S(1)} %get-tuple-element.182), channel_id=1, source_target_pairs={{0,6},{2,4},{4,2},{6,0},{8,14},{10,12},{12,10},{14,8},{1,7},{3,5},... | collective-permute-start | bytes 196616 | tf_op jit(solution)/shard_map/cond/branch_2_fun/ppermute | solution.py:453
  6.2 4.3 %collective-permute-start.9 = (bf16[64,512]{1,0:T(8,128)(2,1)S(1)}, bf16[64,512]{1,0:T(8,128)(2,1)S(1)}, u32[]{:S(2)}, u32[]{:S(2)}) collective-permute-start(bf16[64,512]{1,0:T(8,128)(2,1)S(1)} %get-tuple-element.183), channel_id=1, source_target_pairs={{0,2},{2,0},{4,6},{6,4},{8,10},{10,8},{12,14},{14,12},{1,3},{3,1},... | collective-permute-start | bytes 196616 | tf_op jit(solution)/shard_map/cond/branch_2_fun/ppermute | solution.py:453
  6.7 4.3 %collective-permute-start.10 = (bf16[64,512]{1,0:T(8,128)(2,1)S(1)}, bf16[64,512]{1,0:T(8,128)(2,1)S(1)}, u32[]{:S(2)}, u32[]{:S(2)}) collective-permute-start(bf16[64,512]{1,0:T(8,128)(2,1)S(1)} %get-tuple-element.184), channel_id=1, source_target_pairs={{0,4},{2,6},{4,0},{6,2},{8,12},{10,14},{12,8},{14,10},{1,5},{3,7},... | collective-permute-start | bytes 196616 | tf_op jit(solution)/shard_map/cond/branch_2_fun/ppermute | solution.py:453
  11.1 5.6 %collective-permute-start.11 = (bf16[48,512]{1,0:T(8,128)(2,1)S(1)}, bf16[48,512]{1,0:T(8,128)(2,1)S(1)}, u32[]{:S(2)}, u32[]{:S(2)}) collective-permute-start(bf16[48,512]{1,0:T(8,128)(2,1)S(1)} %get-tuple-element.196), channel_id=1, source_target_pairs={{0,8},{2,10},{4,12},{6,14},{8,0},{10,2},{12,4},{14,6},{1,9},{3,11}... | collective-permute-start | bytes 147464 | tf_op jit(solution)/shard_map/cond/branch_2_fun/ppermute | solution.py:453

commit v3 on v2

--- a/solution.py
+++ b/solution.py
@@ -36,7 +36,7 @@
 
 def step_sizes(page_total, reqs):
     most = (page_total - 1, min(page_total, page_total // 4 + reqs - 1))
-    usual = [(3, 2), (3, 3), (4, 3), (4, 4)]
+    usual = [(3, 2), (3, 3), (4, 2), (4, 3), (5, 4)]
     return [u for u in usual if u[0] < most[0] and u[1] <= most[1]] + [most]
 
 
@@ -114,28 +114,23 @@
         own_ref[:, kind * cols : (kind + 1) * cols] = totals[kind].astype(jnp.bfloat16)
     if sizes:
 
-        def pack(largest, chosen):
-            for j in range(largest):
+        def pack(pages, chosen):
+            for j in range(pages):
                 at = slice(j * page, (j + 1) * page)
-                cuts = [
-                    own_ref[pl.ds(pl.multiple_of(lists[i][j] * page, page), page), :]
-                    for i in range(4)
-                ]
-                keep_ref[at, :] = cuts[0]
-                for i, send in chosen:
-                    if send.shape[0] > j * page:
-                        send[at, :] = cuts[1 + i % 3]
-
-        last = len(sizes) - 1
-        all_sends = list(enumerate(sends))
-        if last:
-            pl.when(choice_ref[0] < last)(lambda: pack(max(u[0] for u in sizes[:last]), all_sends[:-3]))
-        pl.when(choice_ref[0] == last)(lambda: pack(sizes[last][0], all_sends[-3:]))
+                for i, out in enumerate([keep_ref] + chosen):
+                    begin = pl.multiple_of(lists[i][j] * page, page)
+                    out[at, :] = own_ref[pl.ds(begin, page), :]
+
+        firsts = [first for first, _ in sizes]
+        for k, first in enumerate(sorted(set(firsts))):
+            places = [i for i, other in enumerate(firsts) if other == first]
+            chosen = (choice_ref[0] >= places[0]) & (choice_ref[0] <= places[-1])
+            pl.when(chosen)(functools.partial(pack, first, list(sends[3 * k : 3 * k + 3])))
 
 
 def project(hidden, weight, owner, reqs, page, sizes):
     tokens, cols = hidden.shape[1], weight.shape[2]
-    pieces = max(1, hidden.shape[0] // 128)
+    pieces = max(1, hidden.shape[0] // 512)
     rows = lambda n: jax.ShapeDtypeStruct((n * page, 2 * cols), jnp.bfloat16)
     scratch = [
         pltpu.VMEM(hidden.shape, jnp.bfloat16),
@@ -373,18 +368,25 @@
             [rows_kv, jnp.zeros((tokens - rows_kv.shape[0], 2 * width), jnp.bfloat16)], axis=0
         )
     k, v = rows_kv[:, :width], rows_kv[:, width:]
-    s = (dot_nt(q_ref[...], k) * SCALE).reshape(reqs, rows // 8, 8, tokens) + bias_ref[...][:, None]
-    s = s.reshape(reqs * rows, tokens)
-    m_old = m_ref[...]
-    m = jnp.maximum(m_old, jnp.max(s, axis=1, keepdims=True))
-    alpha = jnp.exp2(m_old - m)
-    p_new = jnp.exp2(s - m[:, :1])
-    l = l_ref[...] * alpha + jnp.sum(p_new, axis=1, keepdims=True)
-    pv = jnp.dot(p_new.astype(jnp.bfloat16), v, preferred_element_type=jnp.float32)
     part = rows // groups
-    pv = pv.reshape(reqs, groups, part, width)
-    pv = jnp.stack([pv[:, g, :, g * HEAD_DIM : (g + 1) * HEAD_DIM] for g in range(groups)], axis=1)
-    of[...] = (o_ref[...] * alpha + pv.reshape(reqs * rows, HEAD_DIM)) / l
+
+    def of_group(x, g):
+        return x.reshape(reqs, groups, part, x.shape[1])[:, g].reshape(reqs * part, x.shape[1])
+
+    for g in range(groups):
+        at = slice(g * HEAD_DIM, (g + 1) * HEAD_DIM)
+        s = dot_nt(of_group(q_ref[:, at], g), k[:, at]) * SCALE
+        s = s.reshape(reqs, part // 8, 8, tokens) + bias_ref[...][:, None]
+        s = s.reshape(reqs * part, tokens)
+        m_old = of_group(m_ref[...], g)
+        m = jnp.maximum(m_old, jnp.max(s, axis=1, keepdims=True))
+        alpha = jnp.exp2(m_old - m)
+        p_new = jnp.exp2(s - m[:, :1])
+        l = of_group(l_ref[...], g) * alpha + jnp.sum(p_new, axis=1, keepdims=True)
+        pv = jnp.dot(p_new.astype(jnp.bfloat16), v[:, at], preferred_element_type=jnp.float32)
+        out = (of_group(o_ref[...], g) * alpha + pv) / l
+        for r in range(reqs):
+            of[r * rows + g * part : r * rows + (g + 1) * part, :] = out[r * part : (r + 1) * part]
     copies = []
     for r in range(reqs):
         for g in range(groups):

time: 17.6 us -> 17 us (0.966); the launches traced: 17.9 us -> 16.8 us
  waiting for transfers between devices: 3.89 us -> 3.02 us
  Pallas kernels: 6.62 us -> 6.37 us
    ppermute x4, waiting for transfers between devices: 3.89 us -> 3.02 us  [trade(): return lax.ppermute(x, 'pool', [(i, i ^ bits) for i in range(pool)])]
    pallas_call x1, Pallas kernels: 2.1 us -> 1.67 us  [project(): pl.pallas_call(functools.partial(project_kernel, pieces, reqs, page, size...]
    pallas_call x1, Pallas kernels: 1.17 us -> 1.37 us  [prompt(): pl.pallas_call(functools.partial(prompt_kernel, reqs, steps, groups, len(...]
  transfers between devices with their start and end apart: 4 -> 4, of which waited for: 3 -> 3; matrix products, arithmetic and copies ran while one was open for 0% -> 0% of each run, Pallas kernels for 18% -> 19%
where the time goes in v3:
time: 17 us; the launch traced here: 16.8 us
  starting transfers between devices  7.31 us (43%)
  Pallas kernels  6.37 us (37%)
  waiting for transfers between devices  3.02 us (18%)
    ppermute x4, starting transfers between devices, trade(): return lax.ppermute(x, 'pool', [(i, i ^ bits) for i in range(pool)])  7.31 us
    pallas_call x1, Pallas kernels, cached(): pl.pallas_call(functools.partial(cached_kernel, reqs, steps, groups, page...  3.17 us
    ppermute x4, waiting for transfers between devices, trade(): return lax.ppermute(x, 'pool', [(i, i ^ bits) for i in range(pool)])  3.02 us
    pallas_call x1, Pallas kernels, project(): pl.pallas_call(functools.partial(project_kernel, pieces, reqs, page, size...  1.67 us
    pallas_call x1, Pallas kernels, prompt(): pl.pallas_call(functools.partial(prompt_kernel, reqs, steps, groups, len(...  1.37 us
  transfers between devices with their start and end apart: 4, of which 3 were waited for; matrix products, arithmetic and copies ran while one was open for 0% of the time, Pallas kernels for 19%

profile of v3, /device:TPU:0, one launch (start us, length us, event | category | flops | bytes accessed | tf_op | source)
XLA Modules:
  0.0 16.8 jit_solution(13206467458641414504)
XLA Ops:
  0.0 1.7 %project.1 = (bf16[48,512]{1,0:T(8,128)(2,1)S(1)}, bf16[48,512]{1,0:T(8,128)(2,1)S(1)}, bf16[48,512]{1,0:T(8,128)(2,1)S(1)}, bf16[64,512]{1,0:T(8,128)(2,1)S(1)}...) custom-call(bf16[1024,128]{1,0:T(8,128)(2,1)} %hidden_ref.1, ...), custom_call_target="tpu_custom_call" | custom-call | flops 134217728 | bytes 1441792 | tf_op jit(solution)/shard_map/project/pallas_call | solution.py:154
  1.7 15.1 %conditional.1 = (bf16[4,4,2048]{2,1,0:T(4,128)(2,1)}) conditional(s32[]{:T(128)} %clamp.3, (bf16[48,512]{1,0:T(8,128)(2,1)S(1)}, bf16[48,512]{1,0:T(8,128)(2,1)S(1)}, bf16[48,512]{1,0:T(8,128)(2,1)S(1)}, s32[4,64]{1,0:T(4,128)}, s32[4]{0:T(128)}, /*index=5*/s32[8]{0:T(128)}, s32[4]{0:T(128)}, ...), branch_computations={%region_0.0_spmd, %region_1.0_spmd, %region_2.0_spmd, %region_3.0_... | conditional | flops 286785536 | bytes 6357160 | solution.py:465
  1.7 4.0 %collective-permute-start = (bf16[48,512]{1,0:T(8,128)(2,1)S(1)}, bf16[48,512]{1,0:T(8,128)(2,1)S(1)}, u32[]{:S(2)}, u32[]{:S(2)}) collective-permute-start(bf16[48,512]{1,0:T(8,128)(2,1)S(1)} %get-tuple-element.142), channel_id=1, source_target_pairs={{0,6},{2,4},{4,2},{6,0},{8,14},{10,12},{12,10},{14,8},{1,7},{3,5},... | collective-permute-start | bytes 147464 | tf_op jit(solution)/shard_map/cond/branch_0_fun/ppermute | solution.py:455
  5.7 0.5 %collective-permute-start.1 = (bf16[48,512]{1,0:T(8,128)(2,1)S(1)}, bf16[48,512]{1,0:T(8,128)(2,1)S(1)}, u32[]{:S(2)}, u32[]{:S(2)}) collective-permute-start(bf16[48,512]{1,0:T(8,128)(2,1)S(1)} %get-tuple-element.168), channel_id=1, source_target_pairs={{0,2},{2,0},{4,6},{6,4},{8,10},{10,8},{12,14},{14,12},{1,3},{3,1},... | collective-permute-start | bytes 147464 | tf_op jit(solution)/shard_map/cond/branch_0_fun/ppermute | solution.py:455
  6.3 0.1 collective-permute-start.2
  6.4 3.2 %cached.6 = (bf16[256,256]{1,0:T(8,128)(2,1)S(1)}, f32[256,128]{1,0:T(8,128)S(1)}, f32[256,128]{1,0:T(8,128)S(1)}, f32[256,128]{1,0:T(8,128)S(1)}, f32[4,8,128]{2,1,0:T(8,128)S(1)}) custom-call(s32[4,64]{1,0:T(4,128)} %get-tuple-element.174.table_hbm, s32[4]{0:T(128)} %get-tuple-element.175.len_hbm, s32[8]{0:T(128)} %get-tuple-element.176.owner_hbm, ...), custom_call_target="tpu_custom_call" | custom-call | flops 268435456 | bytes 4194304 | tf_op jit(solution)/shard_map/cond/branch_0_fun/cached/pallas_call | solution.py:319
  9.5 0.0 collective-permute-done.refs_0_
  9.5 0.3 %collective-permute-done.1.refs_1_ = bf16[48,512]{1,0:T(8,128)(2,1)S(1)} collective-permute-done((bf16[48,512]{1,0:T(8,128)(2,1)S(1)}, bf16[48,512]{1,0:T(8,128)(2,1)S(1)}, u32[]{:S(2)}, u32[]{:S(2)}) %collective-permute-start.1) | collective-permute-done | bytes 49184 | tf_op jit(solution)/shard_map/cond/branch_0_fun/ppermute | solution.py:455
  9.8 0.5 %collective-permute-done.2.refs_2_ = bf16[48,512]{1,0:T(8,128)(2,1)S(1)} collective-permute-done((bf16[48,512]{1,0:T(8,128)(2,1)S(1)}, bf16[48,512]{1,0:T(8,128)(2,1)S(1)}, u32[]{:S(2)}, u32[]{:S(2)}) %collective-permute-start.2) | collective-permute-done | bytes 49184 | tf_op jit(solution)/shard_map/cond/branch_0_fun/ppermute | solution.py:455
  10.3 0.2 fold.6
  10.5 2.7 %collective-permute-start.3 = (bf16[32,512]{1,0:T(8,128)(2,1)S(1)}, bf16[32,512]{1,0:T(8,128)(2,1)S(1)}, u32[]{:S(2)}, u32[]{:S(2)}) collective-permute-start(bf16[32,512]{1,0:T(8,128)(2,1)S(1)} %get-tuple-element.183), channel_id=1, source_target_pairs={{0,8},{2,10},{4,12},{6,14},{8,0},{10,2},{12,4},{14,6},{1,9},{3,11}... | collective-permute-start | bytes 98312 | tf_op jit(solution)/shard_map/cond/branch_0_fun/ppermute | solution.py:455
  13.2 2.2 %collective-permute-done.3.refs_1_ = bf16[32,512]{1,0:T(8,128)(2,1)S(1)} collective-permute-done((bf16[32,512]{1,0:T(8,128)(2,1)S(1)}, bf16[32,512]{1,0:T(8,128)(2,1)S(1)}, u32[]{:S(2)}, u32[]{:S(2)}) %collective-permute-start.3) | collective-permute-done | bytes 32800 | tf_op jit(solution)/shard_map/cond/branch_0_fun/ppermute | solution.py:455
  15.4 1.4 %prompt.6 = bf16[4,4,2048]{2,1,0:T(4,128)(2,1)} custom-call(bf16[32,512]{1,0:T(8,128)(2,1)S(1)} %get-tuple-element.182.refs_0_, bf16[32,512]{1,0:T(8,128)(2,1)S(1)} %collective-permute-done.3.refs_1_, bf16[256,256]{1,0:T(8,128)(2,1)S(1)} %get-tuple-element.184.refs_2_, f32[256,128]{1,0:T(8,128)S(1)} %get-tuple-element.185.refs_3_, ...), custom_call_target="tpu_custom_call" | custom-call | tf_op jit(solution)/shard_map/cond/branch_0_fun/prompt/pallas_call | solution.py:408
Async XLA Ops:
  1.7 7.8 %collective-permute-start = (bf16[48,512]{1,0:T(8,128)(2,1)S(1)}, bf16[48,512]{1,0:T(8,128)(2,1)S(1)}, u32[]{:S(2)}, u32[]{:S(2)}) collective-permute-start(bf16[48,512]{1,0:T(8,128)(2,1)S(1)} %get-tuple-element.142), channel_id=1, source_target_pairs={{0,6},{2,4},{4,2},{6,0},{8,14},{10,12},{12,10},{14,8},{1,7},{3,5},... | collective-permute-start | bytes 147464 | tf_op jit(solution)/shard_map/cond/branch_0_fun/ppermute | solution.py:455
  5.7 4.1 %collective-permute-start.1 = (bf16[48,512]{1,0:T(8,128)(2,1)S(1)}, bf16[48,512]{1,0:T(8,128)(2,1)S(1)}, u32[]{:S(2)}, u32[]{:S(2)}) collective-permute-start(bf16[48,512]{1,0:T(8,128)(2,1)S(1)} %get-tuple-element.168), channel_id=1, source_target_pairs={{0,2},{2,0},{4,6},{6,4},{8,10},{10,8},{12,14},{14,12},{1,3},{3,1},... | collective-permute-start | bytes 147464 | tf_op jit(solution)/shard_map/cond/branch_0_fun/ppermute | solution.py:455
  6.3 4.1 %collective-permute-start.2 = (bf16[48,512]{1,0:T(8,128)(2,1)S(1)}, bf16[48,512]{1,0:T(8,128)(2,1)S(1)}, u32[]{:S(2)}, u32[]{:S(2)}) collective-permute-start(bf16[48,512]{1,0:T(8,128)(2,1)S(1)} %get-tuple-element.170), channel_id=1, source_target_pairs={{0,4},{2,6},{4,0},{6,2},{8,12},{10,14},{12,8},{14,10},{1,5},{3,7},... | collective-permute-start | bytes 147464 | tf_op jit(solution)/shard_map/cond/branch_0_fun/ppermute | solution.py:455
  10.5 4.9 %collective-permute-start.3 = (bf16[32,512]{1,0:T(8,128)(2,1)S(1)}, bf16[32,512]{1,0:T(8,128)(2,1)S(1)}, u32[]{:S(2)}, u32[]{:S(2)}) collective-permute-start(bf16[32,512]{1,0:T(8,128)(2,1)S(1)} %get-tuple-element.183), channel_id=1, source_target_pairs={{0,8},{2,10},{4,12},{6,14},{8,0},{10,2},{12,4},{14,6},{1,9},{3,11}... | collective-permute-start | bytes 98312 | tf_op jit(solution)/shard_map/cond/branch_0_fun/ppermute | solution.py:455
